TPU v7x, 32 devices: a whole 2x2x4 slice. The times are simulated.
32 devices in a mesh: lat: 8 (over z, core), lon: 4 (over y, x).
Axes of the slice: x: 2, y: 2, z: 4, core: 2. Of those that a mesh axis runs over, the one named last changes fastest.
Arguments:
- features: bfloat16 [32, 2048, 256], P('lat', 'lon'), may hold values from -6 to 6
- basis: float32 [32, 9, 25], P('lat'), may hold values from -1.2 to 1.2
- span_lo: int32 [32], P('lat'), may hold values from -2 to 0
- span_hi: int32 [32], P('lat'), may hold values from 0 to 2
- weight: bfloat16 [9, 256, 256], replicated, may hold values from -0.125 to 0.125
- cotangent: bfloat16 [32, 2048, 256], P('lat', 'lon'), may hold values from -6 to 6
Outputs:
- mixed: bfloat16 [32, 2048, 256], P('lat', 'lon')
- grad_input: bfloat16 [32, 2048, 256], P('lat', 'lon')
- grad_weight: float32 [9, 256, 256], replicated
All inputs are finite; a program needn't handle non-finite values.
Results may differ from a plain program's by a relative error of at most 0.0049.
Values may be sent and summed in bfloat16 or wider, within the bound.
A program may use at most 192 MiB of HBM per device.

v0:
```python
import math

import jax
import jax.numpy as jnp
from jax import lax
from jax.sharding import PartitionSpec as P

K = 9
RAD = 2
TAPS = 25


def extended_2(block, sides, width, periodic):
    for axis, dim in sides:
        count = lax.axis_size(axis)
        forward = [(i, i + 1) for i in range(count - 1)]
        if periodic:
            forward.append((count - 1, 0))
        backward = [(target, source) for source, target in forward]
        low = lax.ppermute(
            lax.slice_in_dim(block, block.shape[dim] - width, None, axis=dim), axis, forward
        )
        high = lax.ppermute(lax.slice_in_dim(block, 0, width, axis=dim), axis, backward)
        block = jnp.concatenate([low, block, high], axis=dim)
    return block


def from_behind(block, axis, distance):
    devices = range(lax.axis_size(axis))
    route = [((i - distance) % len(devices), i) for i in devices]
    return lax.ppermute(block, axis, route)


def passed_along(block, axis, distance):
    devices = range(lax.axis_size(axis))
    route = [(i - distance, i) for i in devices if i - distance in devices]
    return lax.ppermute(block, axis, route)


def kept_basis(basis, span_lo, span_hi):
    offsets = jnp.arange(TAPS, dtype=jnp.int32) // (2 * RAD + 1) - RAD
    keep = (offsets[None, :] >= span_lo[:, None]) & (offsets[None, :] <= span_hi[:, None])
    return jnp.where(keep[:, None, :], basis, jnp.zeros_like(basis))


def tap_shifts(tap_index):
    return (tap_index // (2 * RAD + 1) - RAD, tap_index % (2 * RAD + 1) - RAD)


def basis_planes(extended, kept, row_count, lon_count):
    planes = []
    for kernel in range(K):
        total = jnp.zeros((row_count, lon_count, extended.shape[2]), jnp.float32)
        for tap_index in range(TAPS):
            row_shift, col_shift = tap_shifts(tap_index)
            window = extended[
                RAD + row_shift : RAD + row_shift + row_count,
                RAD + col_shift : RAD + col_shift + lon_count,
            ]
            total = total + kept[:, kernel, tap_index][:, None, None] * window.astype(jnp.float32)
        planes.append(total.astype(jnp.bfloat16))
    return jnp.stack(planes)


def per_device(features, basis, span_lo, span_hi, weight, cotangent):
    row_count, lon_count, channels = features.shape
    kept = kept_basis(basis, span_lo, span_hi)
    feat_ext = extended_2(features, (("lon", 1),), RAD, True)
    feat_ext = extended_2(feat_ext, (("lat", 0),), RAD, False)
    planes = basis_planes(feat_ext, kept, row_count, lon_count)
    mixed = jnp.einsum("krjc,kco->rjo", planes, weight, preferred_element_type=jnp.float32).astype(
        jnp.bfloat16
    )
    local_grad = jnp.einsum("krjc,rjo->kco", planes, cotangent, preferred_element_type=jnp.float32)
    summed = lax.psum(local_grad, ("lat", "lon"))
    scale = 1.0 / math.sqrt(row_count * lax.axis_size("lat") * lon_count * lax.axis_size("lon"))
    grad_weight = summed * scale
    grad_planes = jnp.einsum("rjo,kco->krjc", cotangent, weight, preferred_element_type=jnp.float32)
    grad_planes = grad_planes.astype(jnp.bfloat16)
    width = 2 * RAD + 1
    spread = jnp.zeros((row_count + 2 * RAD, lon_count + 2 * RAD, channels), jnp.float32)
    for row_index in range(width):
        row_shift = row_index - RAD
        line = jnp.zeros((row_count, lon_count + 2 * RAD, channels), jnp.float32)
        for col_index in range(width):
            tap_index = row_index * width + col_index
            col_shift = col_index - RAD
            term = jnp.zeros((row_count, lon_count, channels), jnp.float32)
            for kernel in range(K):
                term = term + kept[:, kernel, tap_index][:, None, None] * grad_planes[
                    kernel
                ].astype(jnp.float32)
            line = line + jnp.pad(term, ((0, 0), (RAD + col_shift, RAD - col_shift), (0, 0)))
        spread = spread + jnp.pad(line, ((RAD + row_shift, RAD - row_shift), (0, 0), (0, 0)))
    core = spread[:, RAD : RAD + lon_count]
    for by_step in (1, -1):
        if by_step == 1:
            border = spread[:, lon_count + RAD :]
        else:
            border = spread[:, :RAD]
        moved = from_behind(border, "lon", by_step)
        if by_step == 1:
            core = jnp.concatenate([core[:, :RAD] + moved, core[:, RAD:]], axis=1)
        else:
            core = jnp.concatenate(
                [core[:, : lon_count - RAD], core[:, lon_count - RAD :] + moved], axis=1
            )
    middle = core[RAD : RAD + row_count]
    for by_step in (1, -1):
        if by_step == 1:
            border = core[row_count + RAD :]
        else:
            border = core[:RAD]
        moved = passed_along(border, "lat", by_step)
        if by_step == 1:
            middle = jnp.concatenate([middle[:RAD] + moved, middle[RAD:]], axis=0)
        else:
            middle = jnp.concatenate(
                [middle[: row_count - RAD], middle[row_count - RAD :] + moved], axis=0
            )
    grad_input = middle.astype(jnp.bfloat16)
    return (mixed, grad_input, grad_weight)


def solution(mesh):
    return jax.shard_map(
        per_device,
        mesh=mesh,
        in_specs=(
            P("lat", "lon", None),
            P("lat", None, None),
            P("lat"),
            P("lat"),
            P(),
            P("lat", "lon", None),
        ),
        out_specs=(P("lat", "lon", None), P("lat", "lon", None), P()),
        check_vma=False,
    )
```

profile of v0, /device:TPU:0, one launch (start us, length us, event | category | flops | bytes accessed | tf_op | source)
XLA Modules:
  0.0 363.0 jit_solution(13008963595192534351)
XLA Ops:
  7.2 0.8 compare_and_fusion
  8.1 0.7 broadcast_select_fusion
  10.3 1.0 slice_reduce_fusion.174
  11.4 1.1 slice_reduce_fusion.173
  12.4 1.0 slice_reduce_fusion.199
  14.5 1.1 slice_reduce_fusion.99
  16.2 1.1 slice_reduce_fusion.149
  17.3 1.0 slice_reduce_fusion.95
  18.3 3.9 %convert_bitcast_fusion = bf16[9,4,512,256]{3,2,1,0:T(8,128)(2,1)S(1)} fusion(bf16[9,256,256]{2,1,0:T(8,128)(2,1)S(1)} %copy-done, bf16[4,512,256]{2,1,0:T(8,128)(2,1)} %param.11), kind=kOutput, calls=%fused_computation.225 | convolution fusion | flops 2420637696 | bytes 11665408 | tf_op jit(solution)/shard_map/rjo,kco->krjc/dot_general | solution.py:78
  22.2 2.8 fusion.224
  25.1 2.6 fusion.232
  27.8 2.6 fusion.240
  30.4 2.6 fusion.248
  33.1 2.6 fusion.256
  35.7 0.8 pad_add_fusion.5
  36.5 3.6 fusion.344
  40.1 3.6 fusion.352
  43.8 3.6 fusion.360
  47.3 3.6 fusion.368
  50.9 3.6 fusion.376
  54.5 4.0 %fusion.384 = f32[4,512,256]{2,1,0:T(8,128)} fusion(f32[4]{0:T(128)S(1)} %get-tuple-element.8, f32[4]{0:T(128)S(1)} %get-tuple-element.32, f32[4]{0:T(128)S(1)} %get-tuple-element.57, f32[4]{0:T(128)S(1)} %get-tuple-element.102, f32[4]{0:T(128)S(1)} %get-tuple-element.86, f32[4]{0:T(128)S(1)} %get-tuple-element.132, f32[4]{0:T(128)S(1)} %get-tuple-element.158, ...), kind=kLoop, calls=%fused_computation.843 | loop fusion | flops 13631488 | bytes 11534480 | tf_op jit(solution)/shard_map/add | solution.py:90
  58.5 3.6 fusion.392
  62.1 3.6 fusion.400
  65.7 3.6 fusion.408
  69.3 3.5 fusion.416
  72.8 2.6 fusion.336
  75.5 2.6 fusion.272
  78.1 2.6 fusion.280
  80.8 2.6 fusion.288
  83.5 2.7 fusion.296
  86.2 1.9 fusion.304
  88.3 3.1 fusion.312
  91.4 2.9 fusion.320
  94.5 2.9 fusion.328
  97.4 2.9 fusion.264
  100.3 8.0 %pad_add_fusion.1 = (f32[4,516,256]{2,1,0:T(8,128)S(1)}, f32[4,516,256]{2,1,0:T(8,128)S(1)}) fusion(f32[4,512,256]{2,1,0:T(8,128)} %fusion.416, f32[4,512,256]{2,1,0:T(8,128)} %fusion.408, f32[4,512,256]{2,1,0:T(8,128)} %fusion.400, f32[4,512,256]{2,1,0:T(8,128)} %fusion.392, f32[4,512,256]{2,1,0:T(8,128)} %fusion.384, f32[4,512,256]{2,1,0:T(8,128)} %fusion.376, ...), kind=kLoop, calls=%fused_computation.455 | loop fusion | flops 4227072 | bytes 25198592 | tf_op jit(solution)/shard_map/add | solution.py:93
  108.6 3.8 %pad_add_fusion.3 = (f32[4,516,256]{2,1,0:T(8,128)S(1)}, f32[4,516,256]{2,1,0:T(8,128)S(1)}) fusion(f32[4,512,256]{2,1,0:T(8,128)S(1)} %fusion.336, f32[4,512,256]{2,1,0:T(8,128)} %fusion.328, f32[4,512,256]{2,1,0:T(8,128)S(1)} %copy-done.4, f32[4,512,256]{2,1,0:T(8,128)S(1)} %copy-done.3, f32[4,512,256]{2,1,0:T(8,128)S(1)} %fusion.304, ...), kind=kLoop, calls=%fused_computation.457 | loop fusion | flops 4227072 | bytes 25198592 | tf_op jit(solution)/shard_map/add | solution.py:93
  112.4 3.9 %collective-permute-start.5 = (f32[8,2,256]{2,1,0:T(2,128)S(1)}, f32[8,2,256]{2,1,0:T(2,128)S(1)}, u32[]{:S(2)}, u32[]{:S(2)}) collective-permute-start(f32[8,2,256]{2,1,0:T(2,128)S(1)} %pad_add_fusion.6), channel_id=1, source_target_pairs={{1,0},{2,1},{3,2},{0,3},{5,4},{6,5},{7,6},{4,7},{9,8},{10,9},{11,1... | collective-permute-start | bytes 49160 | tf_op jit(solution)/shard_map/ppermute | solution.py:31
  116.6 2.7 collective-permute-start.1
  119.3 1.1 pad_add_fusion
  121.6 1.3 collective-permute-start.2
  123.4 1.3 collective-permute-start.3
  124.7 2.0 collective-permute-start.4
  126.8 2.7 collective-permute-done.4
  130.0 4.0 %collective-permute-start.6 = (f32[2,512,256]{2,1,0:T(8,128)S(1)}, f32[2,512,256]{2,1,0:T(8,128)S(1)}, u32[]{:S(2)}, u32[]{:S(2)}) collective-permute-start(f32[2,512,256]{2,1,0:T(8,128)S(1)} %slice.2014), channel_id=1, source_target_pairs={{0,4},{4,8},{8,12},{12,16},{16,20},{20,24},{24,28},{1,5},{5,9},{9,... | collective-permute-start | bytes 3145736 | tf_op jit(solution)/shard_map/ppermute | solution.py:37
  134.3 1.1 maximum_maximum_fusion
  135.5 8.0 %bitcast_dynamic-update-slice_fusion.7 = (bf16[9,4,512,256]{3,2,0,1:T(8,128)(2,1)S(1)}, bf16[4,512,256]{2,1,0:T(8,128)(2,1)S(1)}) fusion(f32[4]{0:T(128)} %get-tuple-element.203, f32[4]{0:T(128)} %get-tuple-element.204, f32[4]{0:T(128)} %get-tuple-element.205, f32[4]{0:T(128)} %get-tuple-element.206, f32[4]{0:T(128)} %get-tuple-element.207, ...), kind=kLoop, calls=%fused_computation.919 | loop fusion | flops 42991616 | bytes 26218896
  143.6 7.8 %bitcast_dynamic-update-slice_fusion.6 = bf16[9,4,512,256]{3,2,0,1:T(8,128)(2,1)S(1)} fusion(bf16[9,4,512,256]{3,2,0,1:T(8,128)(2,1)S(1)} %get-tuple-element.228, f32[4]{0:T(128)} %get-tuple-element.178, f32[4]{0:T(128)} %get-tuple-element.179, f32[4]{0:T(128)} %get-tuple-element.180, f32[4]{0:T(128)} %get-tuple-element.181, f32[4]{0:T(128)} %get-tuple-element.182, ...), kind=kLoop, calls=%fused_computation.918 | loop fusion | flops 40894464 | bytes 26221376
  151.6 7.6 %bitcast_dynamic-update-slice_fusion.5 = bf16[9,4,512,256]{3,2,0,1:T(8,128)(2,1)S(1)} fusion(bf16[9,4,512,256]{3,2,0,1:T(8,128)(2,1)S(1)} %bitcast_dynamic-update-slice_fusion.6, f32[4]{0:T(128)} %get-tuple-element.153, f32[4]{0:T(128)} %get-tuple-element.154, f32[4]{0:T(128)} %get-tuple-element.155, f32[4]{0:T(128)} %get-tuple-element.156, ...), kind=kLoop, calls=%fused_computation.917 | loop fusion | flops 40894464 | bytes 26229312
  159.4 7.7 %bitcast_dynamic-update-slice_fusion.4 = bf16[9,4,512,256]{3,2,0,1:T(8,128)(2,1)S(1)} fusion(bf16[9,4,512,256]{3,2,0,1:T(8,128)(2,1)S(1)} %bitcast_dynamic-update-slice_fusion.5, f32[4]{0:T(128)S(1)} %get-tuple-element.128, f32[4]{0:T(128)S(1)} %get-tuple-element.129, f32[4]{0:T(128)S(1)} %get-tuple-element.130, f32[4]{0:T(128)S(1)} %get-tuple-element.131, ...), kind=kLoop, calls=%fused_computation.916 | loop fusion | flops 40894464 | bytes 26226336
  167.2 7.6 %bitcast_dynamic-update-slice_fusion.3 = bf16[9,4,512,256]{3,2,0,1:T(8,128)(2,1)S(1)} fusion(bf16[9,4,512,256]{3,2,0,1:T(8,128)(2,1)S(1)} %bitcast_dynamic-update-slice_fusion.4, f32[4]{0:T(128)S(1)} %copy-done.73, f32[4]{0:T(128)S(1)} %copy-done.75, f32[4]{0:T(128)S(1)} %copy-done.77, f32[4]{0:T(128)S(1)} %copy-done.79, f32[4]{0:T(128)S(1)} %copy-done.81, ...), kind=kLoop, calls=%fused_computation.915 | loop fusion | flops 40894464 | bytes 26230304
  174.9 7.7 %bitcast_dynamic-update-slice_fusion.2 = bf16[9,4,512,256]{3,2,0,1:T(8,128)(2,1)S(1)} fusion(bf16[9,4,512,256]{3,2,0,1:T(8,128)(2,1)S(1)} %bitcast_dynamic-update-slice_fusion.3, f32[4]{0:T(128)S(1)} %get-tuple-element.78, f32[4]{0:T(128)S(1)} %get-tuple-element.99, f32[4]{0:T(128)S(1)} %get-tuple-element.100, f32[4]{0:T(128)S(1)} %get-tuple-element.101, ...), kind=kLoop, calls=%fused_computation.914 | loop fusion | flops 40894464 | bytes 26230800
  182.7 6.8 %bitcast_dynamic-update-slice_fusion.1 = bf16[9,4,512,256]{3,2,0,1:T(8,128)(2,1)S(1)} fusion(bf16[9,4,512,256]{3,2,0,1:T(8,128)(2,1)S(1)} %bitcast_dynamic-update-slice_fusion.2, f32[4]{0:T(128)S(1)} %get-tuple-element.53, f32[4]{0:T(128)S(1)} %get-tuple-element.54, f32[4]{0:T(128)S(1)} %get-tuple-element.55, f32[4]{0:T(128)S(1)} %get-tuple-element.56, ...), kind=kLoop, calls=%fused_computation.913 | loop fusion | flops 40894464 | bytes 26231296
  189.7 6.8 %bitcast_dynamic-update-slice_fusion = bf16[9,4,512,256]{3,2,0,1:T(8,128)(2,1)S(1)} fusion(bf16[9,4,512,256]{3,2,0,1:T(8,128)(2,1)S(1)} %bitcast_dynamic-update-slice_fusion.1, f32[4]{0:T(128)S(1)} %get-tuple-element.28, f32[4]{0:T(128)S(1)} %get-tuple-element.29, f32[4]{0:T(128)S(1)} %get-tuple-element.30, f32[4]{0:T(128)S(1)} %get-tuple-element.31, ...), kind=kLoop, calls=%fused_computation.912 | loop fusion | flops 40894464 | bytes 26231296
  196.6 6.8 %bitcast_dynamic-update-slice_fusion.8 = bf16[9,4,512,256]{3,2,0,1:T(8,128)(2,1)S(1)} fusion(bf16[9,4,512,256]{3,2,0,1:T(8,128)(2,1)S(1)} %bitcast_dynamic-update-slice_fusion, f32[4]{0:T(128)S(1)} %get-tuple-element.4, f32[4]{0:T(128)S(1)} %get-tuple-element.5, f32[4]{0:T(128)S(1)} %get-tuple-element.6, f32[4]{0:T(128)S(1)} %get-tuple-element.7, ...), kind=kLoop, calls=%fused_computation.921 | loop fusion | flops 40894464 | bytes 26231296 | tf_op jit(solution)/shard_map/stack | solution.py:62
  203.5 3.6 copy-done.6
  207.1 4.2 %convolution_bitcast_fusion = f32[9,256,256]{2,1,0:T(8,128)} fusion(bf16[9,4,512,256]{3,2,0,1:T(8,128)(2,1)S(1)} %bitcast_dynamic-update-slice_fusion.8, bf16[4,512,256]{2,1,0:T(8,128)(2,1)S(1)} %copy-done.5), kind=kOutput, calls=%fused_computation.886 | convolution fusion | flops 2415919104 | bytes 12845056 | tf_op jit(solution)/shard_map/krjc,rjo->kco/dot_general | solution.py:74
  211.3 2.7 fusion.430
  214.0 1.6 collective-permute-start.7
  215.6 7.3 %bitcast_convert_fusion = bf16[4,512,256]{2,1,0:T(8,128)(2,1)} fusion(bf16[9,4,512,256]{3,2,0,1:T(8,128)(2,1)} %copy-done.6, bf16[9,256,256]{2,1,0:T(8,128)(2,1)S(1)} %copy-done), kind=kOutput, calls=%fused_computation.876 | convolution fusion | flops 2416443392 | bytes 11665408 | tf_op jit(solution)/shard_map/krjc,kco->rjo/dot_general | solution.py:71
  222.8 127.1 %all-reduce.32.cloned.1.call-done = f32[9,256,256]{2,1,0:T(8,128)} async-done(((f32[9,256,256]{2,1,0:T(8,128)}), f32[9,256,256]{2,1,0:T(8,128)}) %all-reduce.32.cloned.1.call-update) | async-done | bytes 2359312 | tf_op jit(solution)/shard_map/psum | solution.py:75
  350.0 3.3 broadcast_multiply_fusion
  353.2 1.3 fusion.429
  354.6 1.1 pad_maximum_fusion.3
  (295 shorter events, 6.4 us)
Async XLA Ops:
  7.2 11.1 %copy-start = (bf16[9,256,256]{2,1,0:T(8,128)(2,1)S(1)}, bf16[9,256,256]{2,1,0:T(8,128)(2,1)}, u32[]{:S(2)}) copy-start(bf16[9,256,256]{2,1,0:T(8,128)(2,1)} %param.10) | copy-start | bytes 3538948
  7.2 342.8 %all-reduce.32.cloned.1.call-start = ((), (), s32[]{:S(2)}) async-start(), calls=%async_computation | async-start | bytes 4718592 | tf_op jit(solution)/shard_map/psum | solution.py:75
  9.8 12.4 %copy-start.7 = (f32[4]{0:T(128)}, f32[4]{0:T(128)S(1)}, u32[]{:S(2)}) copy-start(f32[4]{0:T(128)S(1)} %get-tuple-element.3) | copy-start | bytes 52
  9.8 26.7 %copy-start.13 = (f32[4]{0:T(128)}, f32[4]{0:T(128)S(1)}, u32[]{:S(2)}) copy-start(f32[4]{0:T(128)S(1)} %get-tuple-element.13) | copy-start | bytes 52
  9.8 30.3 %copy-start.11 = (f32[4]{0:T(128)}, f32[4]{0:T(128)S(1)}, u32[]{:S(2)}) copy-start(f32[4]{0:T(128)S(1)} %get-tuple-element.12) | copy-start | bytes 52
  9.8 33.9 %copy-start.9 = (f32[4]{0:T(128)}, f32[4]{0:T(128)S(1)}, u32[]{:S(2)}) copy-start(f32[4]{0:T(128)S(1)} %get-tuple-element.11) | copy-start | bytes 52
  11.3 19.0 %copy-start.60 = (f32[4]{0:T(128)}, f32[4]{0:T(128)S(1)}, u32[]{:S(2)}) copy-start(f32[4]{0:T(128)S(1)} %get-tuple-element.175) | copy-start | bytes 52
  11.3 21.7 %copy-start.58 = (f32[4]{0:T(128)}, f32[4]{0:T(128)S(1)}, u32[]{:S(2)}) copy-start(f32[4]{0:T(128)S(1)} %get-tuple-element.174) | copy-start | bytes 52
  11.3 61.5 %copy-start.41 = (f32[4]{0:T(128)}, f32[4]{0:T(128)S(1)}, u32[]{:S(2)}) copy-start(f32[4]{0:T(128)S(1)} %get-tuple-element.164) | copy-start | bytes 52
  11.3 64.1 %copy-start.54 = (f32[4]{0:T(128)}, f32[4]{0:T(128)S(1)}, u32[]{:S(2)}) copy-start(f32[4]{0:T(128)S(1)} %get-tuple-element.172) | copy-start | bytes 52
  11.3 66.8 %copy-start.52 = (f32[4]{0:T(128)}, f32[4]{0:T(128)S(1)}, u32[]{:S(2)}) copy-start(f32[4]{0:T(128)S(1)} %get-tuple-element.171) | copy-start | bytes 52
  11.3 69.4 %copy-start.50 = (f32[4]{0:T(128)}, f32[4]{0:T(128)S(1)}, u32[]{:S(2)}) copy-start(f32[4]{0:T(128)S(1)} %get-tuple-element.170) | copy-start | bytes 52
  11.4 72.1 %copy-start.48 = (f32[4]{0:T(128)}, f32[4]{0:T(128)S(1)}, u32[]{:S(2)}) copy-start(f32[4]{0:T(128)S(1)} %get-tuple-element.169) | copy-start | bytes 52
  12.4 12.6 %copy-start.68 = (f32[4]{0:T(128)}, f32[4]{0:T(128)S(1)}, u32[]{:S(2)}) copy-start(f32[4]{0:T(128)S(1)} %get-tuple-element.176) | copy-start | bytes 52
  12.4 15.3 %copy-start.70 = (f32[4]{0:T(128)}, f32[4]{0:T(128)S(1)}, u32[]{:S(2)}) copy-start(f32[4]{0:T(128)S(1)} %get-tuple-element.177) | copy-start | bytes 52
  14.0 11.1 %copy-start.15 = (f32[4]{0:T(128)}, f32[4]{0:T(128)S(1)}, u32[]{:S(2)}) copy-start(f32[4]{0:T(128)S(1)} %get-tuple-element.22) | copy-start | bytes 52
  14.0 13.7 %copy-start.21 = (f32[4]{0:T(128)}, f32[4]{0:T(128)S(1)}, u32[]{:S(2)}) copy-start(f32[4]{0:T(128)S(1)} %get-tuple-element.27) | copy-start | bytes 52
  14.0 16.4 %copy-start.19 = (f32[4]{0:T(128)}, f32[4]{0:T(128)S(1)}, u32[]{:S(2)}) copy-start(f32[4]{0:T(128)S(1)} %get-tuple-element.26) | copy-start | bytes 52
  14.0 19.0 %copy-start.17 = (f32[4]{0:T(128)}, f32[4]{0:T(128)S(1)}, u32[]{:S(2)}) copy-start(f32[4]{0:T(128)S(1)} %get-tuple-element.25) | copy-start | bytes 52
  14.5 10.5 %copy-start.29 = (f32[4]{0:T(128)}, f32[4]{0:T(128)S(1)}, u32[]{:S(2)}) copy-start(f32[4]{0:T(128)S(1)} %get-tuple-element.77) | copy-start | bytes 52
  14.5 13.2 %copy-start.27 = (f32[4]{0:T(128)}, f32[4]{0:T(128)S(1)}, u32[]{:S(2)}) copy-start(f32[4]{0:T(128)S(1)} %get-tuple-element.76) | copy-start | bytes 52
  14.5 15.9 %copy-start.25 = (f32[4]{0:T(128)}, f32[4]{0:T(128)S(1)}, u32[]{:S(2)}) copy-start(f32[4]{0:T(128)S(1)} %get-tuple-element.75) | copy-start | bytes 52
  15.6 9.5 %copy-start.66 = (f32[4]{0:T(128)}, f32[4]{0:T(128)S(1)}, u32[]{:S(2)}) copy-start(f32[4]{0:T(128)S(1)} %get-tuple-element.81) | copy-start | bytes 52
  15.6 12.1 %copy-start.64 = (f32[4]{0:T(128)}, f32[4]{0:T(128)S(1)}, u32[]{:S(2)}) copy-start(f32[4]{0:T(128)S(1)} %get-tuple-element.80) | copy-start | bytes 52
  15.6 20.9 %copy-start.90 = (f32[4]{0:T(128)}, f32[4]{0:T(128)S(1)}, u32[]{:S(2)}) copy-start(f32[4]{0:T(128)S(1)} %get-tuple-element.91) | copy-start | bytes 52
  15.6 24.5 %copy-start.88 = (f32[4]{0:T(128)}, f32[4]{0:T(128)S(1)}, u32[]{:S(2)}) copy-start(f32[4]{0:T(128)S(1)} %get-tuple-element.90) | copy-start | bytes 52
  15.6 28.1 %copy-start.86 = (f32[4]{0:T(128)}, f32[4]{0:T(128)S(1)}, u32[]{:S(2)}) copy-start(f32[4]{0:T(128)S(1)} %get-tuple-element.89) | copy-start | bytes 52
  15.6 31.7 %copy-start.84 = (f32[4]{0:T(128)}, f32[4]{0:T(128)S(1)}, u32[]{:S(2)}) copy-start(f32[4]{0:T(128)S(1)} %get-tuple-element.88) | copy-start | bytes 52
  15.6 35.3 %copy-start.82 = (f32[4]{0:T(128)}, f32[4]{0:T(128)S(1)}, u32[]{:S(2)}) copy-start(f32[4]{0:T(128)S(1)} %get-tuple-element.87) | copy-start | bytes 52
  15.6 38.8 %copy-start.80 = (f32[4]{0:T(128)}, f32[4]{0:T(128)S(1)}, u32[]{:S(2)}) copy-start(f32[4]{0:T(128)S(1)} %get-tuple-element.86) | copy-start | bytes 52
  15.7 42.8 %copy-start.78 = (f32[4]{0:T(128)}, f32[4]{0:T(128)S(1)}, u32[]{:S(2)}) copy-start(f32[4]{0:T(128)S(1)} %get-tuple-element.85) | copy-start | bytes 52
  15.7 46.4 %copy-start.76 = (f32[4]{0:T(128)}, f32[4]{0:T(128)S(1)}, u32[]{:S(2)}) copy-start(f32[4]{0:T(128)S(1)} %get-tuple-element.84) | copy-start | bytes 52
  15.7 50.0 %copy-start.74 = (f32[4]{0:T(128)}, f32[4]{0:T(128)S(1)}, u32[]{:S(2)}) copy-start(f32[4]{0:T(128)S(1)} %get-tuple-element.83) | copy-start | bytes 52
  15.7 53.6 %copy-start.72 = (f32[4]{0:T(128)}, f32[4]{0:T(128)S(1)}, u32[]{:S(2)}) copy-start(f32[4]{0:T(128)S(1)} %get-tuple-element.82) | copy-start | bytes 52
  16.2 8.9 %copy-start.39 = (f32[4]{0:T(128)}, f32[4]{0:T(128)S(1)}, u32[]{:S(2)}) copy-start(f32[4]{0:T(128)S(1)} %get-tuple-element.52) | copy-start | bytes 52
  16.2 11.6 %copy-start.37 = (f32[4]{0:T(128)}, f32[4]{0:T(128)S(1)}, u32[]{:S(2)}) copy-start(f32[4]{0:T(128)S(1)} %get-tuple-element.51) | copy-start | bytes 52
  16.2 14.2 %copy-start.35 = (f32[4]{0:T(128)}, f32[4]{0:T(128)S(1)}, u32[]{:S(2)}) copy-start(f32[4]{0:T(128)S(1)} %get-tuple-element.50) | copy-start | bytes 52
  16.2 16.9 %copy-start.33 = (f32[4]{0:T(128)}, f32[4]{0:T(128)S(1)}, u32[]{:S(2)}) copy-start(f32[4]{0:T(128)S(1)} %get-tuple-element.49) | copy-start | bytes 52
  100.3 8.0 %copy-start.3 = (f32[4,512,256]{2,1,0:T(8,128)S(1)}, f32[4,512,256]{2,1,0:T(8,128)}, u32[]{:S(2)}) copy-start(f32[4,512,256]{2,1,0:T(8,128)} %fusion.312) | copy-start | bytes 6291460
  100.3 8.3 %copy-start.4 = (f32[4,512,256]{2,1,0:T(8,128)S(1)}, f32[4,512,256]{2,1,0:T(8,128)}, u32[]{:S(2)}) copy-start(f32[4,512,256]{2,1,0:T(8,128)} %fusion.320) | copy-start | bytes 6291460
  112.4 12.3 %collective-permute-start.5 = (f32[8,2,256]{2,1,0:T(2,128)S(1)}, f32[8,2,256]{2,1,0:T(2,128)S(1)}, u32[]{:S(2)}, u32[]{:S(2)}) collective-permute-start(f32[8,2,256]{2,1,0:T(2,128)S(1)} %pad_add_fusion.6), channel_id=1, source_target_pairs={{1,0},{2,1},{3,2},{0,3},{5,4},{6,5},{7,6},{4,7},{9,8},{10,9},{11,1... | collective-permute-start | bytes 49160 | tf_op jit(solution)/shard_map/ppermute | solution.py:31
  116.3 4.6 %collective-permute-start = (bf16[4,2,256]{2,1,0:T(2,128)(2,1)S(1)}, bf16[4,2,256]{2,1,0:T(2,128)(2,1)S(1)}, u32[]{:S(2)}, u32[]{:S(2)}) collective-permute-start(bf16[4,2,256]{2,1,0:T(2,128)(2,1)S(1)} %get-tuple-element.239), channel_id=1, source_target_pairs={{0,1},{1,2},{2,3},{3,0},{4,5},{5,6},{6,7},{7,4},{8,9},{9,10},{10,1... | collective-permute-start | bytes 12296 | tf_op jit(solution)/shard_map/ppermute | solution.py:20
  116.6 4.3 %collective-permute-start.1 = (bf16[4,2,256]{2,1,0:T(2,128)(2,1)S(1)}, bf16[4,2,256]{2,1,0:T(2,128)(2,1)S(1)}, u32[]{:S(2)}, u32[]{:S(2)}) collective-permute-start(bf16[4,2,256]{2,1,0:T(2,128)(2,1)S(1)} %get-tuple-element.238), channel_id=1, source_target_pairs={{1,0},{2,1},{3,2},{0,3},{5,4},{6,5},{7,6},{4,7},{9,8},{10,9},{11,1... | collective-permute-start | bytes 12296 | tf_op jit(solution)/shard_map/ppermute | solution.py:23
  121.6 12.4 %collective-permute-start.2 = (bf16[2,516,256]{2,0,1:T(2,128)(2,1)S(1)}, bf16[2,516,256]{2,0,1:T(2,128)(2,1)S(1)}, u32[]{:S(2)}, u32[]{:S(2)}) collective-permute-start(bf16[2,516,256]{2,0,1:T(2,128)(2,1)S(1)} %copy.19), channel_id=1, source_target_pairs={{0,4},{4,8},{8,12},{12,16},{16,20},{20,24},{24,28},{1,5},{5,9},{9,... | collective-permute-start | bytes 1585160 | tf_op jit(solution)/shard_map/ppermute | solution.py:20
  123.4 10.7 %collective-permute-start.3 = (bf16[2,516,256]{2,0,1:T(2,128)(2,1)S(1)}, bf16[2,516,256]{2,0,1:T(2,128)(2,1)S(1)}, u32[]{:S(2)}, u32[]{:S(2)}) collective-permute-start(bf16[2,516,256]{2,0,1:T(2,128)(2,1)S(1)} %copy.21), channel_id=1, source_target_pairs={{4,0},{8,4},{12,8},{16,12},{20,16},{24,20},{28,24},{5,1},{9,5},{13... | collective-permute-start | bytes 1585160 | tf_op jit(solution)/shard_map/ppermute | solution.py:23
  124.7 4.7 %collective-permute-start.4 = (f32[8,2,256]{2,1,0:T(2,128)S(1)}, f32[8,2,256]{2,1,0:T(2,128)S(1)}, u32[]{:S(2)}, u32[]{:S(2)}) collective-permute-start(f32[8,2,256]{2,1,0:T(2,128)S(1)} %get-tuple-element.231), channel_id=1, source_target_pairs={{3,0},{0,1},{1,2},{2,3},{7,4},{4,5},{5,6},{6,7},{11,8},{8,9},{9,10... | collective-permute-start | bytes 49160 | tf_op jit(solution)/shard_map/ppermute | solution.py:31
  130.0 81.3 %collective-permute-start.6 = (f32[2,512,256]{2,1,0:T(8,128)S(1)}, f32[2,512,256]{2,1,0:T(8,128)S(1)}, u32[]{:S(2)}, u32[]{:S(2)}) collective-permute-start(f32[2,512,256]{2,1,0:T(8,128)S(1)} %slice.2014), channel_id=1, source_target_pairs={{0,4},{4,8},{8,12},{12,16},{16,20},{20,24},{24,28},{1,5},{5,9},{9,... | collective-permute-start | bytes 3145736 | tf_op jit(solution)/shard_map/ppermute | solution.py:37
  135.4 8.0 %copy-start.101 = (f32[4]{0:T(128)S(1)}, f32[4]{0:T(128)}, u32[]{:S(2)}) copy-start(f32[4]{0:T(128)} %get-tuple-element.189) | copy-start | bytes 52
  135.4 8.0 %copy-start.103 = (f32[4]{0:T(128)S(1)}, f32[4]{0:T(128)}, u32[]{:S(2)}) copy-start(f32[4]{0:T(128)} %get-tuple-element.190) | copy-start | bytes 52
  135.4 8.0 %copy-start.105 = (f32[4]{0:T(128)S(1)}, f32[4]{0:T(128)}, u32[]{:S(2)}) copy-start(f32[4]{0:T(128)} %get-tuple-element.191) | copy-start | bytes 52
  135.4 8.0 %copy-start.107 = (f32[4]{0:T(128)S(1)}, f32[4]{0:T(128)}, u32[]{:S(2)}) copy-start(f32[4]{0:T(128)} %get-tuple-element.192) | copy-start | bytes 52
  135.5 8.0 %copy-start.109 = (f32[4]{0:T(128)S(1)}, f32[4]{0:T(128)}, u32[]{:S(2)}) copy-start(f32[4]{0:T(128)} %get-tuple-element.198) | copy-start | bytes 52
  143.5 7.9 %copy-start.42 = (f32[4]{0:T(128)S(1)}, f32[4]{0:T(128)}, u32[]{:S(2)}) copy-start(f32[4]{0:T(128)} %copy-done.41) | copy-start | bytes 52
  143.5 7.9 %copy-start.47 = (f32[4]{0:T(128)S(1)}, f32[4]{0:T(128)}, u32[]{:S(2)}) copy-start(f32[4]{0:T(128)} %get-tuple-element.168) | copy-start | bytes 52
  143.5 7.9 %copy-start.49 = (f32[4]{0:T(128)S(1)}, f32[4]{0:T(128)}, u32[]{:S(2)}) copy-start(f32[4]{0:T(128)} %copy-done.48) | copy-start | bytes 52
  143.5 7.9 %copy-start.51 = (f32[4]{0:T(128)S(1)}, f32[4]{0:T(128)}, u32[]{:S(2)}) copy-start(f32[4]{0:T(128)} %copy-done.50) | copy-start | bytes 52
  143.5 7.9 %copy-start.53 = (f32[4]{0:T(128)S(1)}, f32[4]{0:T(128)}, u32[]{:S(2)}) copy-start(f32[4]{0:T(128)} %copy-done.52) | copy-start | bytes 52
  143.5 7.9 %copy-start.55 = (f32[4]{0:T(128)S(1)}, f32[4]{0:T(128)}, u32[]{:S(2)}) copy-start(f32[4]{0:T(128)} %copy-done.54) | copy-start | bytes 52
  143.5 7.9 %copy-start.57 = (f32[4]{0:T(128)S(1)}, f32[4]{0:T(128)}, u32[]{:S(2)}) copy-start(f32[4]{0:T(128)} %get-tuple-element.173) | copy-start | bytes 52
  143.6 7.9 %copy-start.59 = (f32[4]{0:T(128)S(1)}, f32[4]{0:T(128)}, u32[]{:S(2)}) copy-start(f32[4]{0:T(128)} %copy-done.58) | copy-start | bytes 52
  143.6 7.9 %copy-start.61 = (f32[4]{0:T(128)S(1)}, f32[4]{0:T(128)}, u32[]{:S(2)}) copy-start(f32[4]{0:T(128)} %copy-done.60) | copy-start | bytes 52
  143.6 7.9 %copy-start.69 = (f32[4]{0:T(128)S(1)}, f32[4]{0:T(128)}, u32[]{:S(2)}) copy-start(f32[4]{0:T(128)} %copy-done.68) | copy-start | bytes 52
  196.6 10.5 %copy-start.5 = (bf16[4,512,256]{2,1,0:T(8,128)(2,1)S(1)}, bf16[4,512,256]{2,1,0:T(8,128)(2,1)}, u32[]{:S(2)}) copy-start(bf16[4,512,256]{2,1,0:T(8,128)(2,1)} %param.11) | copy-start | bytes 3145732
  214.0 139.2 %collective-permute-start.7 = (f32[2,512,256]{2,1,0:T(8,128)}, f32[2,512,256]{2,1,0:T(8,128)S(1)}, u32[]{:S(2)}, u32[]{:S(2)}) collective-permute-start(f32[2,512,256]{2,1,0:T(8,128)} %get-tuple-element.233), channel_id=1, source_target_pairs={{4,0},{8,4},{12,8},{16,12},{20,16},{24,20},{28,24},{5,1},{9,5},{13... | collective-permute-start | bytes 3145736 | tf_op jit(solution)/shard_map/ppermute | solution.py:37
  (77 other events, 414.9 us)
Sparse Core Ops, SparseCore 0:
  211.4 138.4 all-reduce.31
where the time goes:
time: 368 us; the launch traced here: 363 us
  other arithmetic  169 us (46%)
  waiting for transfers between devices  130 us (35%)
  starting transfers between devices  17.2 us (5%)
  between operations  16.7 us (5%)
  matrix products  15.4 us (4%)
  local copies, waits for them, and re-layouts  15.1 us (4%)
    psum x1, waiting for transfers between devices, per_device(): summed = lax.psum(local_grad, ('lat', 'lon'))  127 us
    add x25, other arithmetic, per_device(): term + kept[:, kernel, tap_index][:, None, None] * grad_planes[kernel].as...  76.5 us
    unnamed x8, other arithmetic  60 us
    add x3, other arithmetic, per_device(): line + jnp.pad(term, ((0, 0), (RAD + col_shift, RAD - col_shift), (0, 0)))  12.6 us
    slice x12, local copies, waits for them, and re-layouts, basis_planes(): kept[:, kernel, tap_index][:, None, None] * window.astype(jnp.float32)  9.15 us
  transfers between devices with their start and end apart: 9, of which 2 were waited for; matrix products, arithmetic and copies ran while one was open for 24% of the time, Pallas kernels for 0%

commit v1 on v0

v1 whole, which is shorter than its diff:
```python
import functools
import math

import jax
import jax.numpy as jnp
from jax import lax
from jax.experimental import pallas as pl
from jax.experimental.pallas import tpu as pltpu
from jax.sharding import PartitionSpec as P

K = 9
RAD = 2
WIDTH = 2 * RAD + 1
TAPS = WIDTH * WIDTH
J = 32
EDGE = 8
WIN = J + 2 * EDGE


def passed(block, axis, step, periodic):
    count = lax.axis_size(axis)
    route = [(i, (i + step) % count) for i in range(count) if periodic or 0 <= i + step < count]
    return lax.ppermute(block, axis, route)


def extended(block):
    lon_count = block.shape[1]
    low = passed(block[:, lon_count - EDGE :], "lon", 1, True)
    high = passed(block[:, :EDGE], "lon", -1, True)
    block = jnp.concatenate([low, block, high], axis=1)
    above = passed(block[block.shape[0] - RAD :], "lat", 1, False)
    below = passed(block[:RAD], "lat", -1, False)
    return jnp.concatenate([above, block, below], axis=0)


def kept_basis(basis, span_lo, span_hi):
    offsets = jnp.arange(TAPS, dtype=jnp.int32) // WIDTH - RAD
    keep = (offsets[None, :] >= span_lo[:, None]) & (offsets[None, :] <= span_hi[:, None])
    return jnp.where(keep[:, None, :], basis, jnp.zeros_like(basis))


def banded(coef):
    rows = coef.shape[0]
    lane = jnp.arange(WIDTH * WIN)
    spread = jnp.repeat(coef.astype(jnp.bfloat16), WIN, axis=2)
    where_col = lane[None, :] % WIN - jnp.arange(J)[:, None] - (EDGE - RAD)
    out = jnp.zeros((rows, K, J, WIDTH * WIN), jnp.bfloat16)
    for e in range(WIDTH):
        out = jnp.where((where_col == e)[None, None], spread[:, :, None, :, e], out)
    return out.reshape(rows, K * J, WIDTH * WIN)


def kernel(scale, tile, f_ref, c_ref, cot_ref, fa_ref, ca_ref, w_ref, wt_ref, mixed_ref, gi_ref, gw_ref, y_ref, z_ref, acc_ref):
    rows, lon_count, channels = cot_ref.shape
    tiles = lon_count // tile
    acc_ref[...] = jnp.zeros_like(acc_ref)

    def stencil(x_ref, a_ref, out_ref, i, start):
        a = a_ref[i]
        for b in range(tile // J):
            first = pl.multiple_of(start + b * J, J)
            x = x_ref[pl.ds(i, WIDTH), pl.ds(first, WIN), :].reshape(WIDTH * WIN, channels)
            y = jnp.dot(a, x, preferred_element_type=jnp.float32).astype(jnp.bfloat16)
            for k in range(K):
                out_ref[b * J : (b + 1) * J, k * channels : (k + 1) * channels] = y[k * J : (k + 1) * J]

    def step(s, carry):
        i = s // tiles
        start = pl.multiple_of((s % tiles) * tile, tile)
        here = pl.ds(start, tile)
        stencil(f_ref, fa_ref, y_ref, i, start)
        stencil(c_ref, ca_ref, z_ref, i, start)
        mixed_ref[i, here, :] = jnp.dot(
            y_ref[...], w_ref[...], preferred_element_type=jnp.float32
        ).astype(jnp.bfloat16)
        acc_ref[...] += jnp.dot(cot_ref[i, here, :].T, y_ref[...], preferred_element_type=jnp.float32)
        gi_ref[i, here, :] = jnp.dot(
            z_ref[...], wt_ref[...], preferred_element_type=jnp.float32
        ).astype(jnp.bfloat16)
        return carry

    lax.fori_loop(0, rows * tiles, step, 0)
    for k in range(K):
        gw_ref[k] = acc_ref[:, k * channels : (k + 1) * channels].T * scale


def per_device(features, basis, span_lo, span_hi, weight, cotangent):
    rows, lon_count, channels = features.shape
    kept = kept_basis(basis, span_lo, span_hi)
    above = passed(kept[rows - RAD :], "lat", 1, False)
    below = passed(kept[:RAD], "lat", -1, False)
    kept_ext = jnp.concatenate([above, kept, below], axis=0).reshape(rows + 2 * RAD, K, WIDTH, WIDTH)
    forward = banded(kept_ext[RAD : RAD + rows])
    flipped = kept_ext[:, :, ::-1, ::-1]
    adjoint = banded(jnp.stack([flipped[r : r + rows, :, r] for r in range(WIDTH)], axis=2))
    f_ext = extended(features)
    c_ext = extended(cotangent)
    w = weight.reshape(K * channels, channels)
    wt = jnp.swapaxes(weight, 1, 2).reshape(K * channels, channels)
    scale = 1.0 / math.sqrt(rows * lax.axis_size("lat") * lon_count * lax.axis_size("lon"))
    tile = 512
    mixed, grad_input, local = pl.pallas_call(
        functools.partial(kernel, scale, tile),
        out_shape=(
            jax.ShapeDtypeStruct(features.shape, jnp.bfloat16),
            jax.ShapeDtypeStruct(features.shape, jnp.bfloat16),
            jax.ShapeDtypeStruct(weight.shape, jnp.float32),
        ),
        in_specs=[pl.BlockSpec(memory_space=pltpu.VMEM)] * 7,
        out_specs=[pl.BlockSpec(memory_space=pltpu.VMEM)] * 3,
        scratch_shapes=[
            pltpu.VMEM((tile, K * channels), jnp.bfloat16),
            pltpu.VMEM((tile, K * channels), jnp.bfloat16),
            pltpu.VMEM((channels, K * channels), jnp.float32),
        ],
        compiler_params=pltpu.CompilerParams(vmem_limit_bytes=50 * 2**20),
    )(f_ext, c_ext, cotangent, forward, adjoint, w, wt)
    return (mixed, grad_input, lax.psum(local, ("lat", "lon")))


def solution(mesh):
    return jax.shard_map(
        per_device,
        mesh=mesh,
        in_specs=(
            P("lat", "lon", None),
            P("lat", None, None),
            P("lat"),
            P("lat"),
            P(),
            P("lat", "lon", None),
        ),
        out_specs=(P("lat", "lon", None), P("lat", "lon", None), P()),
        check_vma=False,
    )
```

time: 368 us -> 221 us (0.60); the launches traced: 363 us -> 220 us
  other arithmetic: 169 us -> 9.23 us
  Pallas kernels: 0 us -> 17.7 us
  matrix products: 15.4 us -> 0 us
  waiting for transfers between devices: 130 us -> 140 us
  starting transfers between devices: 17.2 us -> 21.9 us
    add x31 -> x0, other arithmetic: 90.2 us -> none  [the longest x25 76.5 us: per_device(): term + kept[:, kernel, tap_index][:, None, None] * grad_planes[kernel].as...]
    unnamed x8 -> x0, other arithmetic: 60 us -> none
    pallas_call x0 -> x1, Pallas kernels: none -> 17.7 us  [per_device(): pl.pallas_call(functools.partial(kernel, scale, tile), out_shape=(jax.Sha...]
    dot_general x3 -> x0, matrix products: 15.4 us -> none  [the longest x1 7.28 us: per_device(): jnp.einsum('krjc,kco->rjo', planes, weight, preferred_element_type=jnp.fl...]
    another operation x3 -> x0, other arithmetic: 10.8 us -> none  [the longest x1 6.83 us: basis_planes(): return jnp.stack(planes)]
    psum x1, waiting for transfers between devices: 127 us -> 136 us  [per_device(): return (mixed, grad_input, lax.psum(local, ('lat', 'lon')))]
    slice x18 -> x6, local copies, waits for them, and re-layouts: 10.5 us -> 4.88 us  [the longest x2 2.69 us: extended(): high = passed(block[:, :EDGE], 'lon', -1, True)]
    ppermute x8 -> x10, starting transfers between devices: 17.1 us -> 21.9 us  [passed(): return lax.ppermute(block, axis, route)]
  transfers between devices with their start and end apart: 9 -> 11, of which waited for: 2 -> 2; matrix products, arithmetic and copies ran while one was open for 24% -> 8% of each run, Pallas kernels for 0% -> 0%
where the time goes in v1:
time: 221 us; the launch traced here: 220 us
  waiting for transfers between devices  140 us (63%)
  starting transfers between devices  21.9 us (10%)
  Pallas kernels  17.7 us (8%)
  local copies, waits for them, and re-layouts  17.2 us (8%)
  between operations  14.4 us (7%)
  other arithmetic  9.23 us (4%)
    psum x1, waiting for transfers between devices, per_device(): return (mixed, grad_input, lax.psum(local, ('lat', 'lon')))  136 us
    ppermute x10, starting transfers between devices, passed(): return lax.ppermute(block, axis, route)  21.9 us
    pallas_call x1, Pallas kernels, per_device(): pl.pallas_call(functools.partial(kernel, scale, tile), out_shape=(jax.Sha...  17.7 us
    concatenate x2, other arithmetic, extended(): return jnp.concatenate([above, block, below], axis=0)  5.72 us
  transfers between devices with their start and end apart: 11, of which 2 were waited for; matrix products, arithmetic and copies ran while one was open for 8% of the time, Pallas kernels for 0%

profile of v1, /device:TPU:0, one launch (start us, length us, event | category | flops | bytes accessed | tf_op | source)
XLA Modules:
  0.0 220.1 jit_solution(2267317880866030161)
XLA Ops:
  7.2 0.0 copy-start
  7.2 0.0 all-reduce.2.cloned.1.call-start
  7.2 0.8 compare_and_fusion
  8.1 0.7 broadcast_select_fusion
  8.8 2.4 %collective-permute-start.8 = (bf16[2,9,25]{2,0,1:T(2,128)(2,1)S(1)}, bf16[2,9,25]{2,0,1:T(2,128)(2,1)S(1)}, u32[]{:S(2)}, u32[]{:S(2)}) collective-permute-start(bf16[2,9,25]{2,0,1:T(2,128)(2,1)S(1)} %get-tuple-element.34), channel_id=1, source_target_pairs={{0,4},{4,8},{8,12},{12,16},{16,20},{20,24},{24,28},{1,5},{5,9},{9,... | collective-permute-start | bytes 2708 | tf_op jit(solution)/shard_map/ppermute | solution.py:23
  11.2 1.3 collective-permute-start.9
  12.5 1.3 fusion.17
  13.8 3.3 %collective-permute-start.1 = (bf16[4,8,256]{2,1,0:T(8,128)(2,1)}, bf16[4,8,256]{2,1,0:T(8,128)(2,1)S(1)}, u32[]{:S(2)}, u32[]{:S(2)}) collective-permute-start(bf16[4,8,256]{2,1,0:T(8,128)(2,1)} %get-tuple-element.15), channel_id=1, source_target_pairs={{0,3},{1,0},{2,1},{3,2},{4,7},{5,4},{6,5},{7,6},{8,11},{9,8},{10,9... | collective-permute-start | bytes 49160 | tf_op jit(solution)/shard_map/ppermute | solution.py:23
  17.1 0.0 collective-permute-start
  17.1 1.3 fusion.16
  18.4 2.9 %collective-permute-start.5 = (bf16[4,8,256]{2,1,0:T(8,128)(2,1)}, bf16[4,8,256]{2,1,0:T(8,128)(2,1)S(1)}, u32[]{:S(2)}, u32[]{:S(2)}) collective-permute-start(bf16[4,8,256]{2,1,0:T(8,128)(2,1)} %get-tuple-element.13), channel_id=1, source_target_pairs={{0,3},{1,0},{2,1},{3,2},{4,7},{5,4},{6,5},{7,6},{8,11},{9,8},{10,9... | collective-permute-start | bytes 49160 | tf_op jit(solution)/shard_map/ppermute | solution.py:23
  21.4 0.1 copy.26
  21.5 0.2 copy.27
  21.8 0.3 broadcast_in_dim.227
  22.0 0.2 reshape.229
  22.3 0.6 fusion.12
  22.9 0.6 copy.29
  23.5 0.0 copy-done
  23.6 0.0 copy-start.4
  23.6 1.5 copy.40
  25.1 0.0 collective-permute-done.8
  25.1 0.0 collective-permute-start.4
  25.1 0.0 collective-permute-done.9
  25.1 0.2 copy.33
  25.4 0.0 collective-permute-done
  25.4 0.0 copy-done.4
  25.4 0.1 constant_dynamic-update-slice_fusion.1
  25.5 0.0 collective-permute-done.1
  25.5 0.0 copy-start.1
  25.5 1.0 fusion.15
  26.6 3.5 %collective-permute-done.4 = bf16[4,8,256]{2,1,0:T(8,128)(2,1)} collective-permute-done((bf16[4,8,256]{2,1,0:T(8,128)(2,1)}, bf16[4,8,256]{2,1,0:T(8,128)(2,1)}, u32[]{:S(2)}, u32[]{:S(2)}) %collective-permute-start.4) | collective-permute-done | bytes 16416 | tf_op jit(solution)/shard_map/ppermute | solution.py:23
  30.1 0.7 constant_dynamic-update-slice_fusion.5
  30.8 0.0 copy-done.1
  30.8 0.1 constant_dynamic-update-slice_fusion.4
  30.8 3.2 %collective-permute-start.2 = (bf16[2,528,256]{2,1,0:T(8,128)(2,1)}, bf16[2,528,256]{2,1,0:T(8,128)(2,1)}, u32[]{:S(2)}, u32[]{:S(2)}) collective-permute-start(bf16[2,528,256]{2,1,0:T(8,128)(2,1)} %get-tuple-element.11), channel_id=1, source_target_pairs={{0,4},{4,8},{8,12},{12,16},{16,20},{20,24},{24,28},{1,5},{5,9},{9,... | collective-permute-start | bytes 1622024 | tf_op jit(solution)/shard_map/ppermute | solution.py:23
  34.1 1.3 collective-permute-start.3
  35.3 0.0 collective-permute-done.5
  35.4 0.0 copy-start.2
  35.4 1.1 fusion.14
  36.5 0.2 copy-done.2
  36.7 6.3 %collective-permute-start.6 = (bf16[2,528,256]{2,1,0:T(8,128)(2,1)}, bf16[2,528,256]{2,1,0:T(8,128)(2,1)}, u32[]{:S(2)}, u32[]{:S(2)}) collective-permute-start(bf16[2,528,256]{2,1,0:T(8,128)(2,1)} %get-tuple-element.9), channel_id=1, source_target_pairs={{0,4},{4,8},{8,12},{12,16},{16,20},{20,24},{24,28},{1,5},{5,9},{9,... | collective-permute-start | bytes 1622024 | tf_op jit(solution)/shard_map/ppermute | solution.py:23
  43.0 1.3 collective-permute-start.7
  44.3 0.2 copy.34
  44.6 1.0 broadcast_in_dim.255
  45.6 1.2 reshape.231
  46.9 0.7 broadcast_in_dim.222
  47.6 0.7 broadcast_in_dim.249
  48.3 0.7 broadcast_in_dim.243
  49.1 1.3 fusion.3
  50.4 0.0 copy-start.3
  50.4 0.0 collective-permute-done.2
  50.4 0.0 collective-permute-done.3
  50.4 2.9 %pad_maximum_fusion.f_ref = bf16[8,528,256]{2,1,0:T(8,128)(2,1)} fusion(bf16[2,528,256]{2,1,0:T(8,128)(2,1)} %collective-permute-done.3, bf16[4,528,256]{2,1,0:T(8,128)(2,1)S(1)} %constant_dynamic-update-slice_fusion, bf16[2,528,256]{2,1,0:T(8,128)(2,1)} %collective-permute-done.2), kind=kLoop, calls=%fused_computation | loop fusion | flops 2162688 | bytes 4325376 | tf_op jit(solution)/shard_map/concatenate | solution.py:33
  53.3 0.0 collective-permute-done.6
  53.3 0.0 collective-permute-done.7
  53.4 0.0 copy-done.3
  53.4 2.8 %pad_maximum_fusion.1.c_ref = bf16[8,528,256]{2,1,0:T(8,128)(2,1)} fusion(bf16[2,528,256]{2,1,0:T(8,128)(2,1)} %collective-permute-done.7, bf16[4,528,256]{2,1,0:T(8,128)(2,1)S(1)} %copy-done.3, bf16[2,528,256]{2,1,0:T(8,128)(2,1)} %collective-permute-done.6), kind=kLoop, calls=%fused_computation.1 | loop fusion | flops 2162688 | bytes 4325376 | tf_op jit(solution)/shard_map/concatenate | solution.py:33
  56.2 17.7 %shard_map.85 = (bf16[4,512,256]{2,1,0:T(8,128)(2,1)}, bf16[4,512,256]{2,1,0:T(8,128)(2,1)}, f32[9,256,256]{2,1,0:T(8,128)}) custom-call(bf16[8,528,256]{2,1,0:T(8,128)(2,1)} %pad_maximum_fusion.f_ref, bf16[8,528,256]{2,1,0:T(8,128)(2,1)} %pad_maximum_fusion.1.c_ref, bf16[4,512,256]{2,1,0:T(8,128)(2,1)S(1)} %copy-done.1, ...), custom_call_target="tpu_custom_call" | custom-call | tf_op jit(solution)/shard_map/pallas_call | solution.py:102
  73.9 0.0 all-reduce.2.cloned.1.call-update
  73.9 136.1 %all-reduce.2.cloned.1.call-done = f32[9,256,256]{2,1,0:T(8,128)} async-done(((f32[9,256,256]{2,1,0:T(8,128)}), f32[9,256,256]{2,1,0:T(8,128)}) %all-reduce.2.cloned.1.call-update) | async-done | bytes 2359312 | tf_op jit(solution)/shard_map/psum | solution.py:118
  210.0 3.2 %copy.50 = f32[9,256,256]{2,1,0:T(8,128)} copy(f32[9,256,256]{2,1,0:T(8,128)} %all-reduce.2.cloned.1.call-done) | data formatting | bytes 4718592
  (26 shorter events, 0.3 us)
Async XLA Ops:
  7.2 16.4 %copy-start = (bf16[9,256,256]{2,1,0:T(8,128)(2,1)S(1)}, bf16[9,256,256]{2,1,0:T(8,128)(2,1)}, u32[]{:S(2)}) copy-start(bf16[9,256,256]{2,1,0:T(8,128)(2,1)} %param.10) | copy-start | bytes 3538948
  7.2 202.8 %all-reduce.2.cloned.1.call-start = ((), (), s32[]{:S(2)}) async-start(), calls=%async_computation | async-start | bytes 4718592 | tf_op jit(solution)/shard_map/psum | solution.py:118
  8.8 16.3 %collective-permute-start.8 = (bf16[2,9,25]{2,0,1:T(2,128)(2,1)S(1)}, bf16[2,9,25]{2,0,1:T(2,128)(2,1)S(1)}, u32[]{:S(2)}, u32[]{:S(2)}) collective-permute-start(bf16[2,9,25]{2,0,1:T(2,128)(2,1)S(1)} %get-tuple-element.34), channel_id=1, source_target_pairs={{0,4},{4,8},{8,12},{12,16},{16,20},{20,24},{24,28},{1,5},{5,9},{9,... | collective-permute-start | bytes 2708 | tf_op jit(solution)/shard_map/ppermute | solution.py:23
  11.2 13.9 %collective-permute-start.9 = (bf16[2,9,25]{2,0,1:T(2,128)(2,1)S(1)}, bf16[2,9,25]{2,0,1:T(2,128)(2,1)S(1)}, u32[]{:S(2)}, u32[]{:S(2)}) collective-permute-start(bf16[2,9,25]{2,0,1:T(2,128)(2,1)S(1)} %get-tuple-element.35), channel_id=1, source_target_pairs={{4,0},{8,4},{12,8},{16,12},{20,16},{24,20},{28,24},{5,1},{9,5},{13... | collective-permute-start | bytes 2708 | tf_op jit(solution)/shard_map/ppermute | solution.py:23
  13.8 11.7 %collective-permute-start.1 = (bf16[4,8,256]{2,1,0:T(8,128)(2,1)}, bf16[4,8,256]{2,1,0:T(8,128)(2,1)S(1)}, u32[]{:S(2)}, u32[]{:S(2)}) collective-permute-start(bf16[4,8,256]{2,1,0:T(8,128)(2,1)} %get-tuple-element.15), channel_id=1, source_target_pairs={{0,3},{1,0},{2,1},{3,2},{4,7},{5,4},{6,5},{7,6},{8,11},{9,8},{10,9... | collective-permute-start | bytes 49160 | tf_op jit(solution)/shard_map/ppermute | solution.py:23
  17.1 8.3 %collective-permute-start = (bf16[4,8,256]{2,1,0:T(8,128)(2,1)S(1)}, bf16[4,8,256]{2,1,0:T(8,128)(2,1)S(1)}, u32[]{:S(2)}, u32[]{:S(2)}) collective-permute-start(bf16[4,8,256]{2,1,0:T(8,128)(2,1)S(1)} %get-tuple-element.16), channel_id=1, source_target_pairs={{0,1},{1,2},{2,3},{3,0},{4,5},{5,6},{6,7},{7,4},{8,9},{9,10},{10,1... | collective-permute-start | bytes 49160 | tf_op jit(solution)/shard_map/ppermute | solution.py:23
  18.4 16.9 %collective-permute-start.5 = (bf16[4,8,256]{2,1,0:T(8,128)(2,1)}, bf16[4,8,256]{2,1,0:T(8,128)(2,1)S(1)}, u32[]{:S(2)}, u32[]{:S(2)}) collective-permute-start(bf16[4,8,256]{2,1,0:T(8,128)(2,1)} %get-tuple-element.13), channel_id=1, source_target_pairs={{0,3},{1,0},{2,1},{3,2},{4,7},{5,4},{6,5},{7,6},{8,11},{9,8},{10,9... | collective-permute-start | bytes 49160 | tf_op jit(solution)/shard_map/ppermute | solution.py:23
  23.6 1.8 copy-start.4
  25.1 5.0 %collective-permute-start.4 = (bf16[4,8,256]{2,1,0:T(8,128)(2,1)}, bf16[4,8,256]{2,1,0:T(8,128)(2,1)}, u32[]{:S(2)}, u32[]{:S(2)}) collective-permute-start(bf16[4,8,256]{2,1,0:T(8,128)(2,1)} %get-tuple-element.14), channel_id=1, source_target_pairs={{0,1},{1,2},{2,3},{3,0},{4,5},{5,6},{6,7},{7,4},{8,9},{9,10},{10,1... | collective-permute-start | bytes 49160 | tf_op jit(solution)/shard_map/ppermute | solution.py:23
  25.5 5.3 %copy-start.1 = (bf16[4,512,256]{2,1,0:T(8,128)(2,1)S(1)}, bf16[4,512,256]{2,1,0:T(8,128)(2,1)}, u32[]{:S(2)}) copy-start(bf16[4,512,256]{2,1,0:T(8,128)(2,1)} %cot_ref.1) | copy-start | bytes 3145732
  30.8 19.6 %collective-permute-start.2 = (bf16[2,528,256]{2,1,0:T(8,128)(2,1)}, bf16[2,528,256]{2,1,0:T(8,128)(2,1)}, u32[]{:S(2)}, u32[]{:S(2)}) collective-permute-start(bf16[2,528,256]{2,1,0:T(8,128)(2,1)} %get-tuple-element.11), channel_id=1, source_target_pairs={{0,4},{4,8},{8,12},{12,16},{16,20},{20,24},{24,28},{1,5},{5,9},{9,... | collective-permute-start | bytes 1622024 | tf_op jit(solution)/shard_map/ppermute | solution.py:23
  34.1 16.4 %collective-permute-start.3 = (bf16[2,528,256]{2,1,0:T(8,128)(2,1)}, bf16[2,528,256]{2,1,0:T(8,128)(2,1)}, u32[]{:S(2)}, u32[]{:S(2)}) collective-permute-start(bf16[2,528,256]{2,1,0:T(8,128)(2,1)} %get-tuple-element.12), channel_id=1, source_target_pairs={{4,0},{8,4},{12,8},{16,12},{20,16},{24,20},{28,24},{5,1},{9,5},{13... | collective-permute-start | bytes 1622024 | tf_op jit(solution)/shard_map/ppermute | solution.py:23
  35.4 1.3 copy-start.2
  36.7 16.6 %collective-permute-start.6 = (bf16[2,528,256]{2,1,0:T(8,128)(2,1)}, bf16[2,528,256]{2,1,0:T(8,128)(2,1)}, u32[]{:S(2)}, u32[]{:S(2)}) collective-permute-start(bf16[2,528,256]{2,1,0:T(8,128)(2,1)} %get-tuple-element.9), channel_id=1, source_target_pairs={{0,4},{4,8},{8,12},{12,16},{16,20},{20,24},{24,28},{1,5},{5,9},{9,... | collective-permute-start | bytes 1622024 | tf_op jit(solution)/shard_map/ppermute | solution.py:23
  43.0 10.4 %collective-permute-start.7 = (bf16[2,528,256]{2,1,0:T(8,128)(2,1)}, bf16[2,528,256]{2,1,0:T(8,128)(2,1)}, u32[]{:S(2)}, u32[]{:S(2)}) collective-permute-start(bf16[2,528,256]{2,1,0:T(8,128)(2,1)} %get-tuple-element.10), channel_id=1, source_target_pairs={{4,0},{8,4},{12,8},{16,12},{20,16},{24,20},{28,24},{5,1},{9,5},{13... | collective-permute-start | bytes 1622024 | tf_op jit(solution)/shard_map/ppermute | solution.py:23
  50.4 3.0 %copy-start.3 = (bf16[4,528,256]{2,1,0:T(8,128)(2,1)S(1)}, bf16[4,528,256]{2,1,0:T(8,128)(2,1)}, u32[]{:S(2)}) copy-start(bf16[4,528,256]{2,1,0:T(8,128)(2,1)} %copy-done.2) | copy-start | bytes 3244036
Sparse Core Ops, SparseCore 0:
  74.0 135.9 all-reduce.1

commit v2 on v1

--- a/solution.py
+++ b/solution.py
@@ -15,6 +15,8 @@
 J = 32
 EDGE = 8
 WIN = J + 2 * EDGE
+SUB, LANES = 16, 128
+MESH = pl.DeviceIdType.MESH
 
 
 def passed(block, axis, step, periodic):
@@ -80,8 +82,152 @@
         return carry
 
     lax.fori_loop(0, rows * tiles, step, 0)
+    per = channels // SUB
     for k in range(K):
-        gw_ref[k] = acc_ref[:, k * channels : (k + 1) * channels].T * scale
+        turned = acc_ref[:, k * channels : (k + 1) * channels].T * scale
+        for h in range(channels // LANES):
+            first = (k * (channels // LANES) + h) * per
+            block = turned[:, h * LANES : (h + 1) * LANES]
+            gw_ref[first : first + per] = block.reshape(per, SUB, LANES)
+    used = K * per * (channels // LANES)
+    if gw_ref.shape[0] > used:
+        gw_ref[used:] = jnp.zeros((gw_ref.shape[0] - used, SUB, LANES), jnp.float32)
+
+
+def reduce_kernel(
+    lon, pairs, q, in_ref, out_ref, got_a, send_b, got_b, part, send_c, got_c,
+    a_send, a_recv, b_send, b_recv, c_send, c_recv, d_send, d_recv, e_send, e_recv, f_send, f_recv,
+):
+    lat = lax.axis_index("lat")
+    n = lax.axis_index("lon")
+    core, z = lax.rem(lat, 2), lat // 2
+    partner = (lat + 1 - 2 * core, n)
+    piece = pairs * q
+    half = lon * piece
+
+    def lon_peer(s):
+        return lax.rem(n + s, lon)
+
+    def pair_peer(s):
+        return lax.rem(z + s, pairs)
+
+    barrier = pltpu.get_barrier_semaphore()
+    pl.semaphore_signal(barrier, inc=1, device_id=partner, device_id_type=MESH)
+    for s in range(1, lon):
+        pl.semaphore_signal(barrier, inc=1, device_id=(lat, lon_peer(s)), device_id_type=MESH)
+    for s in range(1, pairs):
+        pl.semaphore_signal(
+            barrier, inc=1, device_id=(pair_peer(s) * 2 + core, n), device_id_type=MESH
+        )
+    pl.semaphore_wait(barrier, 1 + lon - 1 + pairs - 1)
+
+    def remote(src, dst, send, recv, device):
+        copy = pltpu.make_async_remote_copy(
+            src_ref=src, dst_ref=dst, send_sem=send, recv_sem=recv,
+            device_id=device, device_id_type=MESH,
+        )
+        copy.start()
+        return copy
+
+    theirs, mine = (1 - core) * half, core * half
+    a_copies = []
+    for s in range(lon):
+        p = lon_peer(s + 1)
+        a_copies.append(
+            remote(
+                in_ref.at[pl.ds(theirs + p * piece, piece)],
+                got_a.at[pl.ds(p * piece, piece)],
+                a_send.at[s], a_recv.at[s], partner,
+            )
+        )
+    b_copies = []
+    for s in range(lon):
+        p = lon_peer(s + 1)
+        a_copies[s].wait_recv()
+        total = in_ref[pl.ds(mine + p * piece, piece)] + got_a[pl.ds(p * piece, piece)]
+        if s < lon - 1:
+            send_b[s] = total.astype(jnp.bfloat16)
+            b_copies.append(remote(send_b.at[s], got_b.at[s], b_send.at[s], b_recv.at[s], (lat, p)))
+        else:
+            part[...] = total
+    for s in range(lon - 1):
+        b_copies[s].wait_recv()
+        part[...] += got_b[s].astype(jnp.float32)
+    c_copies = []
+    for s in range(pairs - 1):
+        p = pair_peer(s + 1)
+        send_c[s] = part[pl.ds(p * q, q)].astype(jnp.bfloat16)
+        c_copies.append(
+            remote(send_c.at[s], got_c.at[s], c_send.at[s], c_recv.at[s], (p * 2 + core, n))
+        )
+    total = part[pl.ds(z * q, q)]
+    for s in range(pairs - 1):
+        c_copies[s].wait_recv()
+        total = total + got_c[s].astype(jnp.float32)
+    own = mine + n * piece
+    out_ref[pl.ds(own + z * q, q)] = total.astype(jnp.bfloat16)
+
+    d_copies, e_copies, f_copies = [], [], []
+
+    def to_lon(t):
+        src = out_ref.at[pl.ds(own + lax.rem(z + pairs - t, pairs) * q, q)]
+        for s in range(lon - 1):
+            e_copies.append(
+                remote(src, src, e_send.at[t, s], e_recv.at[t, s], (lat, lon_peer(s + 1)))
+            )
+
+    def to_partner(s, p):
+        src = out_ref.at[pl.ds(mine + p * piece, piece)]
+        f_copies.append(remote(src, src, f_send.at[s], f_recv.at[s], partner))
+
+    src = out_ref.at[pl.ds(own + z * q, q)]
+    for s in range(pairs - 1):
+        d_copies.append(
+            remote(src, src, d_send.at[s], d_recv.at[s], (pair_peer(s + 1) * 2 + core, n))
+        )
+    to_lon(0)
+    for t in range(1, pairs):
+        d_copies[t - 1].wait_recv()
+        to_lon(t)
+    to_partner(0, n)
+    for s in range(lon - 1):
+        for t in range(pairs):
+            e_copies[t * (lon - 1) + s].wait_recv()
+        to_partner(s + 1, lax.rem(n + lon - s - 1, lon))
+    for copy in f_copies:
+        copy.wait_recv()
+    for copy in a_copies + b_copies + c_copies + d_copies + e_copies + f_copies:
+        copy.wait_send()
+
+
+def summed(local, lon, pairs, q):
+    groups = local.shape[0]
+    piece = pairs * q
+    dma = pltpu.SemaphoreType.DMA
+    bf16, f32 = jnp.bfloat16, jnp.float32
+    return pl.pallas_call(
+        functools.partial(reduce_kernel, lon, pairs, q),
+        out_shape=jax.ShapeDtypeStruct((groups, SUB, LANES), bf16),
+        in_specs=[pl.BlockSpec(memory_space=pltpu.VMEM)],
+        out_specs=pl.BlockSpec(memory_space=pltpu.VMEM),
+        scratch_shapes=[
+            pltpu.VMEM((lon * piece, SUB, LANES), f32),
+            pltpu.VMEM((lon - 1, piece, SUB, LANES), bf16),
+            pltpu.VMEM((lon - 1, piece, SUB, LANES), bf16),
+            pltpu.VMEM((piece, SUB, LANES), f32),
+            pltpu.VMEM((pairs - 1, q, SUB, LANES), bf16),
+            pltpu.VMEM((pairs - 1, q, SUB, LANES), bf16),
+            dma((lon,)), dma((lon,)),
+            dma((lon - 1,)), dma((lon - 1,)),
+            dma((pairs - 1,)), dma((pairs - 1,)),
+            dma((pairs - 1,)), dma((pairs - 1,)),
+            dma((pairs, lon - 1)), dma((pairs, lon - 1)),
+            dma((lon,)), dma((lon,)),
+        ],
+        compiler_params=pltpu.CompilerParams(
+            collective_id=1, has_side_effects=True, vmem_limit_bytes=40 * 2**20
+        ),
+    )(local)
 
 
 def per_device(features, basis, span_lo, span_hi, weight, cotangent):
@@ -99,12 +245,15 @@
     wt = jnp.swapaxes(weight, 1, 2).reshape(K * channels, channels)
     scale = 1.0 / math.sqrt(rows * lax.axis_size("lat") * lon_count * lax.axis_size("lon"))
     tile = 512
+    lon, pairs = lax.axis_size("lon"), lax.axis_size("lat") // 2
+    used = weight.size // (SUB * LANES)
+    q = -(-used // (2 * lon * pairs))
     mixed, grad_input, local = pl.pallas_call(
         functools.partial(kernel, scale, tile),
         out_shape=(
             jax.ShapeDtypeStruct(features.shape, jnp.bfloat16),
             jax.ShapeDtypeStruct(features.shape, jnp.bfloat16),
-            jax.ShapeDtypeStruct(weight.shape, jnp.float32),
+            jax.ShapeDtypeStruct((2 * lon * pairs * q, SUB, LANES), jnp.float32),
         ),
         in_specs=[pl.BlockSpec(memory_space=pltpu.VMEM)] * 7,
         out_specs=[pl.BlockSpec(memory_space=pltpu.VMEM)] * 3,
@@ -115,7 +264,10 @@
         ],
         compiler_params=pltpu.CompilerParams(vmem_limit_bytes=50 * 2**20),
     )(f_ext, c_ext, cotangent, forward, adjoint, w, wt)
-    return (mixed, grad_input, lax.psum(local, ("lat", "lon")))
+    total = summed(local, lon, pairs, q)[:used].astype(jnp.float32)
+    total = total.reshape(K, channels // LANES, channels, LANES)
+    grad_weight = jnp.swapaxes(total, 1, 2).reshape(weight.shape)
+    return (mixed, grad_input, grad_weight)
 
 
 def solution(mesh):

time: 221 us -> 103 us (0.47)
  waiting for transfers between devices: 140 us -> 3.52 us
  Pallas kernels: 17.7 us -> 49.1 us
  between operations: 14.4 us -> 0.97 us
    psum x1 -> x0, waiting for transfers between devices: 136 us -> none  [per_device(): return (mixed, grad_input, lax.psum(local, ('lat', 'lon')))]
    pallas_call x0 -> x1, Pallas kernels: none -> 31.4 us  [summed(): pl.pallas_call(functools.partial(reduce_kernel, lon, pairs, q), out_shape...]
  transfers between devices with their start and end apart: 11 -> 10, of which waited for: 2 -> 1; matrix products, arithmetic and copies ran while one was open for 8% -> 18% of each run, Pallas kernels for 0% -> 0%
where the time goes in v2:
time: 103 us
  Pallas kernels  49.1 us (48%)
  starting transfers between devices  21.9 us (21%)
  local copies, waits for them, and re-layouts  16.3 us (16%)
  other arithmetic  10.9 us (11%)
  waiting for transfers between devices  3.52 us (3%)
    pallas_call x1, Pallas kernels, summed(): pl.pallas_call(functools.partial(reduce_kernel, lon, pairs, q), out_shape...  31.4 us
    ppermute x10, starting transfers between devices, passed(): return lax.ppermute(block, axis, route)  21.9 us
    pallas_call x1, Pallas kernels, per_device(): pl.pallas_call(functools.partial(kernel, scale, tile), out_shape=(jax.Sha...  17.7 us
    concatenate x2, other arithmetic, extended(): return jnp.concatenate([above, block, below], axis=0)  5.72 us
    unnamed x20, local copies, waits for them, and re-layouts  3.56 us
    ppermute x10, waiting for transfers between devices, passed(): return lax.ppermute(block, axis, route)  3.52 us
    broadcast_in_dim x17, local copies, waits for them, and re-layouts, banded(): out = jnp.where((where_col == e)[None, None], spread[:, :, None, :, e], out)  2.93 us
    slice x2, local copies, waits for them, and re-layouts, extended(): high = passed(block[:, :EDGE], 'lon', -1, True)  2.69 us
  transfers between devices with their start and end apart: 10, of which 1 were waited for; matrix products, arithmetic and copies ran while one was open for 18% of the time, Pallas kernels for 0%

profile of v2, /device:TPU:0, one launch (start us, length us, event | category | flops | bytes accessed | tf_op | source)
XLA Modules:
  0.0 102.7 jit_solution(9631183646860851054)
XLA Ops:
  0.6 0.0 copy-start
  0.7 0.8 compare_and_fusion
  1.5 0.7 broadcast_select_fusion
  2.2 2.4 %collective-permute-start.8 = (bf16[2,9,25]{2,0,1:T(2,128)(2,1)S(1)}, bf16[2,9,25]{2,0,1:T(2,128)(2,1)S(1)}, u32[]{:S(2)}, u32[]{:S(2)}) collective-permute-start(bf16[2,9,25]{2,0,1:T(2,128)(2,1)S(1)} %get-tuple-element.34), channel_id=1, source_target_pairs={{0,4},{4,8},{8,12},{12,16},{16,20},{20,24},{24,28},{1,5},{5,9},{9,... | collective-permute-start | bytes 2708 | tf_op jit(solution)/shard_map/ppermute | solution.py:25
  4.6 1.3 %collective-permute-start.9 = (bf16[2,9,25]{2,0,1:T(2,128)(2,1)S(1)}, bf16[2,9,25]{2,0,1:T(2,128)(2,1)S(1)}, u32[]{:S(2)}, u32[]{:S(2)}) collective-permute-start(bf16[2,9,25]{2,0,1:T(2,128)(2,1)S(1)} %get-tuple-element.35), channel_id=1, source_target_pairs={{4,0},{8,4},{12,8},{16,12},{20,16},{24,20},{28,24},{5,1},{9,5},{13... | collective-permute-start | bytes 2708 | tf_op jit(solution)/shard_map/ppermute | solution.py:25
  5.9 1.3 %fusion.17 = (bf16[4,8,256]{2,1,0:T(8,128)(2,1)}, bf16[4,8,256]{2,1,0:T(8,128)(2,1)S(1)}) fusion(bf16[4,512,256]{2,1,0:T(8,128)(2,1)} %param.6), kind=kLoop, calls=%fused_computation.58 | loop fusion | bytes 65536 | tf_op jit(solution)/shard_map/slice | solution.py:31
  7.2 3.3 %collective-permute-start.1 = (bf16[4,8,256]{2,1,0:T(8,128)(2,1)}, bf16[4,8,256]{2,1,0:T(8,128)(2,1)S(1)}, u32[]{:S(2)}, u32[]{:S(2)}) collective-permute-start(bf16[4,8,256]{2,1,0:T(8,128)(2,1)} %get-tuple-element.15), channel_id=1, source_target_pairs={{0,3},{1,0},{2,1},{3,2},{4,7},{5,4},{6,5},{7,6},{8,11},{9,8},{10,9... | collective-permute-start | bytes 49160 | tf_op jit(solution)/shard_map/ppermute | solution.py:25
  10.5 0.0 collective-permute-start
  10.5 1.3 %fusion.16 = (bf16[4,8,256]{2,1,0:T(8,128)(2,1)}, bf16[4,8,256]{2,1,0:T(8,128)(2,1)}) fusion(bf16[4,512,256]{2,1,0:T(8,128)(2,1)} %cot_ref.1), kind=kLoop, calls=%fused_computation.57 | loop fusion | bytes 65536 | tf_op jit(solution)/shard_map/slice | solution.py:31
  11.9 2.9 %collective-permute-start.5 = (bf16[4,8,256]{2,1,0:T(8,128)(2,1)}, bf16[4,8,256]{2,1,0:T(8,128)(2,1)S(1)}, u32[]{:S(2)}, u32[]{:S(2)}) collective-permute-start(bf16[4,8,256]{2,1,0:T(8,128)(2,1)} %get-tuple-element.13), channel_id=1, source_target_pairs={{0,3},{1,0},{2,1},{3,2},{4,7},{5,4},{6,5},{7,6},{8,11},{9,8},{10,9... | collective-permute-start | bytes 49160 | tf_op jit(solution)/shard_map/ppermute | solution.py:25
  14.8 0.1 copy.28
  14.9 0.2 copy.29
  15.2 0.3 broadcast_in_dim.227
  15.4 0.2 reshape.239
  15.7 0.6 fusion.12
  16.4 0.6 copy.31
  17.0 0.0 copy-done
  17.0 0.0 copy-start.5
  17.0 1.5 %copy.42 = bf16[9,256,256]{2,1,0:T(8,128)(2,1)} copy(bf16[9,256,256]{1,2,0:T(8,128)(2,1)S(1)} %bitcast.78) | data formatting | bytes 2359296 | tf_op jit(solution)/shard_map/transpose | solution.py:245
  18.5 0.0 collective-permute-done.8
  18.5 0.0 collective-permute-start.4
  18.5 0.0 collective-permute-done.9
  18.6 0.2 copy.35
  18.8 0.0 collective-permute-done
  18.8 0.0 copy-done.5
  18.8 0.1 constant_dynamic-update-slice_fusion.1
  18.9 0.0 copy-start.1
  18.9 0.0 collective-permute-done.1
  18.9 1.0 %fusion.15 = (bf16[2,528,256]{2,1,0:T(8,128)(2,1)}, bf16[2,528,256]{2,1,0:T(8,128)(2,1)}) fusion(bf16[4,528,256]{2,1,0:T(8,128)(2,1)S(1)} %constant_dynamic-update-slice_fusion), kind=kLoop, calls=%fused_computation.56 | loop fusion | bytes 2162688 | tf_op jit(solution)/shard_map/slice | solution.py:33
  20.0 3.5 %collective-permute-done.4 = bf16[4,8,256]{2,1,0:T(8,128)(2,1)} collective-permute-done((bf16[4,8,256]{2,1,0:T(8,128)(2,1)}, bf16[4,8,256]{2,1,0:T(8,128)(2,1)}, u32[]{:S(2)}, u32[]{:S(2)}) %collective-permute-start.4) | collective-permute-done | bytes 16416 | tf_op jit(solution)/shard_map/ppermute | solution.py:25
  23.5 0.7 constant_dynamic-update-slice_fusion.5
  24.2 0.0 copy-done.1
  24.2 0.1 constant_dynamic-update-slice_fusion.4
  24.3 3.2 %collective-permute-start.2 = (bf16[2,528,256]{2,1,0:T(8,128)(2,1)}, bf16[2,528,256]{2,1,0:T(8,128)(2,1)}, u32[]{:S(2)}, u32[]{:S(2)}) collective-permute-start(bf16[2,528,256]{2,1,0:T(8,128)(2,1)} %get-tuple-element.11), channel_id=1, source_target_pairs={{0,4},{4,8},{8,12},{12,16},{16,20},{20,24},{24,28},{1,5},{5,9},{9,... | collective-permute-start | bytes 1622024 | tf_op jit(solution)/shard_map/ppermute | solution.py:25
  27.5 1.3 %collective-permute-start.3 = (bf16[2,528,256]{2,1,0:T(8,128)(2,1)}, bf16[2,528,256]{2,1,0:T(8,128)(2,1)}, u32[]{:S(2)}, u32[]{:S(2)}) collective-permute-start(bf16[2,528,256]{2,1,0:T(8,128)(2,1)} %get-tuple-element.12), channel_id=1, source_target_pairs={{4,0},{8,4},{12,8},{16,12},{20,16},{24,20},{28,24},{5,1},{9,5},{13... | collective-permute-start | bytes 1622024 | tf_op jit(solution)/shard_map/ppermute | solution.py:25
  28.8 0.0 collective-permute-done.5
  28.8 0.0 copy-start.3
  28.8 1.0 copy-done.3
  29.8 1.1 %fusion.14 = (bf16[2,528,256]{2,1,0:T(8,128)(2,1)}, bf16[2,528,256]{2,1,0:T(8,128)(2,1)}) fusion(bf16[4,528,256]{2,1,0:T(8,128)(2,1)S(1)} %constant_dynamic-update-slice_fusion.3), kind=kLoop, calls=%fused_computation.55 | loop fusion | bytes 2162688 | tf_op jit(solution)/shard_map/slice | solution.py:33
  30.8 6.3 %collective-permute-start.6 = (bf16[2,528,256]{2,1,0:T(8,128)(2,1)}, bf16[2,528,256]{2,1,0:T(8,128)(2,1)}, u32[]{:S(2)}, u32[]{:S(2)}) collective-permute-start(bf16[2,528,256]{2,1,0:T(8,128)(2,1)} %get-tuple-element.9), channel_id=1, source_target_pairs={{0,4},{4,8},{8,12},{12,16},{16,20},{20,24},{24,28},{1,5},{5,9},{9,... | collective-permute-start | bytes 1622024 | tf_op jit(solution)/shard_map/ppermute | solution.py:25
  37.1 1.3 %collective-permute-start.7 = (bf16[2,528,256]{2,1,0:T(8,128)(2,1)}, bf16[2,528,256]{2,1,0:T(8,128)(2,1)}, u32[]{:S(2)}, u32[]{:S(2)}) collective-permute-start(bf16[2,528,256]{2,1,0:T(8,128)(2,1)} %get-tuple-element.10), channel_id=1, source_target_pairs={{4,0},{8,4},{12,8},{16,12},{20,16},{24,20},{28,24},{5,1},{9,5},{13... | collective-permute-start | bytes 1622024 | tf_op jit(solution)/shard_map/ppermute | solution.py:25
  38.5 0.2 copy.36
  38.7 1.0 broadcast_in_dim.255
  39.7 1.2 %reshape.241 = bf16[4,9,240,5]{2,0,3,1:T(4,128)(2,1)S(1)} reshape(bf16[4,9,5,48,5]{3,2,0,4,1:T(8,128)(2,1)} %broadcast_in_dim.255) | data formatting | bytes 172800 | tf_op jit(solution)/shard_map/reshape | solution.py:47
  41.0 0.7 broadcast_in_dim.222
  41.8 0.7 broadcast_in_dim.249
  42.5 0.7 broadcast_in_dim.243
  43.3 1.3 %fusion.3 = (bf16[4,288,240]{2,1,0:T(8,128)(2,1)S(1)}, bf16[4,288,240]{2,1,0:T(8,128)(2,1)S(1)}) fusion(pred[288,240]{1,0:T(8,128)(4,1)S(1)} %bitcast.83, pred[288,240]{1,0:T(8,128)(4,1)S(1)} %bitcast.84, pred[288,240]{1,0:T(8,128)(4,1)S(1)} %bitcast.85, pred[288,240]{1,0:T(8,128)(4,1)S(1)} %bitcast.86, pred[288,240]{1,0:T(8,128)(4,1)S(1)} %bitcast.82, ...), kind=kLoop, calls=%fused_computation.8 | loop fusion | flops 2764800 | bytes 1624320 | tf_op jit(solution)/shard_map/jit(_where)/select_n | solution.py:51
  44.5 0.0 copy-start.4
  44.5 0.0 collective-permute-done.2
  44.6 0.0 collective-permute-done.3
  44.6 2.9 %pad_maximum_fusion.f_ref = bf16[8,528,256]{2,1,0:T(8,128)(2,1)} fusion(bf16[2,528,256]{2,1,0:T(8,128)(2,1)} %collective-permute-done.3, bf16[4,528,256]{2,1,0:T(8,128)(2,1)S(1)} %constant_dynamic-update-slice_fusion, bf16[2,528,256]{2,1,0:T(8,128)(2,1)} %collective-permute-done.2), kind=kLoop, calls=%fused_computation.2 | loop fusion | flops 2162688 | bytes 4325376 | tf_op jit(solution)/shard_map/concatenate | solution.py:35
  47.5 0.0 collective-permute-done.6
  47.5 0.0 collective-permute-done.7
  47.5 0.0 copy-done.4
  47.5 2.8 %pad_maximum_fusion.1.c_ref = bf16[8,528,256]{2,1,0:T(8,128)(2,1)} fusion(bf16[2,528,256]{2,1,0:T(8,128)(2,1)} %collective-permute-done.7, bf16[4,528,256]{2,1,0:T(8,128)(2,1)S(1)} %copy-done.4, bf16[2,528,256]{2,1,0:T(8,128)(2,1)} %collective-permute-done.6), kind=kLoop, calls=%fused_computation.3 | loop fusion | flops 2162688 | bytes 4325376 | tf_op jit(solution)/shard_map/concatenate | solution.py:35
  50.3 17.7 %shard_map.85 = (bf16[4,512,256]{2,1,0:T(8,128)(2,1)}, bf16[4,512,256]{2,1,0:T(8,128)(2,1)}, f32[288,16,128]{2,1,0:T(8,128)}) custom-call(bf16[8,528,256]{2,1,0:T(8,128)(2,1)} %pad_maximum_fusion.f_ref, bf16[8,528,256]{2,1,0:T(8,128)(2,1)} %pad_maximum_fusion.1.c_ref, bf16[4,512,256]{2,1,0:T(8,128)(2,1)S(1)} %copy-done.1, ...), custom_call_target="tpu_custom_call" | custom-call | tf_op jit(solution)/shard_map/pallas_call | solution.py:251
  68.0 0.0 copy-start.2
  68.0 1.7 %copy-done.2 = f32[288,16,128]{2,1,0:T(8,128)S(1)} copy-done((f32[288,16,128]{2,1,0:T(8,128)S(1)}, f32[288,16,128]{2,1,0:T(8,128)}, u32[]{:S(2)}) %copy-start.2) | copy-done | bytes 2359320
  69.7 31.4 %shard_map.86 = bf16[288,16,128]{2,1,0:T(8,128)(2,1)S(1)} custom-call(f32[288,16,128]{2,1,0:T(8,128)S(1)} %copy-done.2), custom_call_target="tpu_custom_call" | custom-call | tf_op jit(solution)/shard_map/pallas_call | solution.py:208
  101.1 1.6 %copy_bitcast_fusion = f32[9,256,256]{2,1,0:T(8,128)} fusion(bf16[9,2,256,128]{3,2,1,0:T(8,128)(2,1)S(1)} %bitcast.80), kind=kLoop, calls=%fused_computation | loop fusion | flops 589824 | bytes 3538944 | tf_op jit(solution)/shard_map/reshape | solution.py:269
  (26 shorter events, 0.3 us)
Async XLA Ops:
  0.6 16.4 %copy-start = (bf16[9,256,256]{2,1,0:T(8,128)(2,1)S(1)}, bf16[9,256,256]{2,1,0:T(8,128)(2,1)}, u32[]{:S(2)}) copy-start(bf16[9,256,256]{2,1,0:T(8,128)(2,1)} %param.10) | copy-start | bytes 3538948
  2.2 16.3 %collective-permute-start.8 = (bf16[2,9,25]{2,0,1:T(2,128)(2,1)S(1)}, bf16[2,9,25]{2,0,1:T(2,128)(2,1)S(1)}, u32[]{:S(2)}, u32[]{:S(2)}) collective-permute-start(bf16[2,9,25]{2,0,1:T(2,128)(2,1)S(1)} %get-tuple-element.34), channel_id=1, source_target_pairs={{0,4},{4,8},{8,12},{12,16},{16,20},{20,24},{24,28},{1,5},{5,9},{9,... | collective-permute-start | bytes 2708 | tf_op jit(solution)/shard_map/ppermute | solution.py:25
  4.6 13.9 %collective-permute-start.9 = (bf16[2,9,25]{2,0,1:T(2,128)(2,1)S(1)}, bf16[2,9,25]{2,0,1:T(2,128)(2,1)S(1)}, u32[]{:S(2)}, u32[]{:S(2)}) collective-permute-start(bf16[2,9,25]{2,0,1:T(2,128)(2,1)S(1)} %get-tuple-element.35), channel_id=1, source_target_pairs={{4,0},{8,4},{12,8},{16,12},{20,16},{24,20},{28,24},{5,1},{9,5},{13... | collective-permute-start | bytes 2708 | tf_op jit(solution)/shard_map/ppermute | solution.py:25
  7.2 11.7 %collective-permute-start.1 = (bf16[4,8,256]{2,1,0:T(8,128)(2,1)}, bf16[4,8,256]{2,1,0:T(8,128)(2,1)S(1)}, u32[]{:S(2)}, u32[]{:S(2)}) collective-permute-start(bf16[4,8,256]{2,1,0:T(8,128)(2,1)} %get-tuple-element.15), channel_id=1, source_target_pairs={{0,3},{1,0},{2,1},{3,2},{4,7},{5,4},{6,5},{7,6},{8,11},{9,8},{10,9... | collective-permute-start | bytes 49160 | tf_op jit(solution)/shard_map/ppermute | solution.py:25
  10.5 8.3 %collective-permute-start = (bf16[4,8,256]{2,1,0:T(8,128)(2,1)S(1)}, bf16[4,8,256]{2,1,0:T(8,128)(2,1)S(1)}, u32[]{:S(2)}, u32[]{:S(2)}) collective-permute-start(bf16[4,8,256]{2,1,0:T(8,128)(2,1)S(1)} %get-tuple-element.16), channel_id=1, source_target_pairs={{0,1},{1,2},{2,3},{3,0},{4,5},{5,6},{6,7},{7,4},{8,9},{9,10},{10,1... | collective-permute-start | bytes 49160 | tf_op jit(solution)/shard_map/ppermute | solution.py:25
  11.9 16.9 %collective-permute-start.5 = (bf16[4,8,256]{2,1,0:T(8,128)(2,1)}, bf16[4,8,256]{2,1,0:T(8,128)(2,1)S(1)}, u32[]{:S(2)}, u32[]{:S(2)}) collective-permute-start(bf16[4,8,256]{2,1,0:T(8,128)(2,1)} %get-tuple-element.13), channel_id=1, source_target_pairs={{0,3},{1,0},{2,1},{3,2},{4,7},{5,4},{6,5},{7,6},{8,11},{9,8},{10,9... | collective-permute-start | bytes 49160 | tf_op jit(solution)/shard_map/ppermute | solution.py:25
  17.0 1.8 %copy-start.5 = (bf16[4,512,256]{2,1,0:T(8,128)(2,1)S(1)}, bf16[4,512,256]{2,1,0:T(8,128)(2,1)}, u32[]{:S(2)}) copy-start(bf16[4,512,256]{2,1,0:T(8,128)(2,1)} %param.6) | copy-start | bytes 3145732
  18.5 5.0 %collective-permute-start.4 = (bf16[4,8,256]{2,1,0:T(8,128)(2,1)}, bf16[4,8,256]{2,1,0:T(8,128)(2,1)}, u32[]{:S(2)}, u32[]{:S(2)}) collective-permute-start(bf16[4,8,256]{2,1,0:T(8,128)(2,1)} %get-tuple-element.14), channel_id=1, source_target_pairs={{0,1},{1,2},{2,3},{3,0},{4,5},{5,6},{6,7},{7,4},{8,9},{9,10},{10,1... | collective-permute-start | bytes 49160 | tf_op jit(solution)/shard_map/ppermute | solution.py:25
  18.9 5.3 %copy-start.1 = (bf16[4,512,256]{2,1,0:T(8,128)(2,1)S(1)}, bf16[4,512,256]{2,1,0:T(8,128)(2,1)}, u32[]{:S(2)}) copy-start(bf16[4,512,256]{2,1,0:T(8,128)(2,1)} %cot_ref.1) | copy-start | bytes 3145732
  24.3 20.3 %collective-permute-start.2 = (bf16[2,528,256]{2,1,0:T(8,128)(2,1)}, bf16[2,528,256]{2,1,0:T(8,128)(2,1)}, u32[]{:S(2)}, u32[]{:S(2)}) collective-permute-start(bf16[2,528,256]{2,1,0:T(8,128)(2,1)} %get-tuple-element.11), channel_id=1, source_target_pairs={{0,4},{4,8},{8,12},{12,16},{16,20},{20,24},{24,28},{1,5},{5,9},{9,... | collective-permute-start | bytes 1622024 | tf_op jit(solution)/shard_map/ppermute | solution.py:25
  27.5 17.1 %collective-permute-start.3 = (bf16[2,528,256]{2,1,0:T(8,128)(2,1)}, bf16[2,528,256]{2,1,0:T(8,128)(2,1)}, u32[]{:S(2)}, u32[]{:S(2)}) collective-permute-start(bf16[2,528,256]{2,1,0:T(8,128)(2,1)} %get-tuple-element.12), channel_id=1, source_target_pairs={{4,0},{8,4},{12,8},{16,12},{20,16},{24,20},{28,24},{5,1},{9,5},{13... | collective-permute-start | bytes 1622024 | tf_op jit(solution)/shard_map/ppermute | solution.py:25
  28.8 1.0 copy-start.3
  30.8 16.6 %collective-permute-start.6 = (bf16[2,528,256]{2,1,0:T(8,128)(2,1)}, bf16[2,528,256]{2,1,0:T(8,128)(2,1)}, u32[]{:S(2)}, u32[]{:S(2)}) collective-permute-start(bf16[2,528,256]{2,1,0:T(8,128)(2,1)} %get-tuple-element.9), channel_id=1, source_target_pairs={{0,4},{4,8},{8,12},{12,16},{16,20},{20,24},{24,28},{1,5},{5,9},{9,... | collective-permute-start | bytes 1622024 | tf_op jit(solution)/shard_map/ppermute | solution.py:25
  37.1 10.4 %collective-permute-start.7 = (bf16[2,528,256]{2,1,0:T(8,128)(2,1)}, bf16[2,528,256]{2,1,0:T(8,128)(2,1)}, u32[]{:S(2)}, u32[]{:S(2)}) collective-permute-start(bf16[2,528,256]{2,1,0:T(8,128)(2,1)} %get-tuple-element.10), channel_id=1, source_target_pairs={{4,0},{8,4},{12,8},{16,12},{20,16},{24,20},{28,24},{5,1},{9,5},{13... | collective-permute-start | bytes 1622024 | tf_op jit(solution)/shard_map/ppermute | solution.py:25
  44.5 3.0 %copy-start.4 = (bf16[4,528,256]{2,1,0:T(8,128)(2,1)S(1)}, bf16[4,528,256]{2,1,0:T(8,128)(2,1)}, u32[]{:S(2)}) copy-start(bf16[4,528,256]{2,1,0:T(8,128)(2,1)} %copy-done.3) | copy-start | bytes 3244036
  68.0 1.7 %copy-start.2 = (f32[288,16,128]{2,1,0:T(8,128)S(1)}, f32[288,16,128]{2,1,0:T(8,128)}, u32[]{:S(2)}) copy-start(f32[288,16,128]{2,1,0:T(8,128)} %get-tuple-element.8.in_ref) | copy-start | bytes 7077892

commit v3 on v2

v3 whole, which is shorter than its diff:
```python
import functools
import math

import jax
import jax.numpy as jnp
from jax import lax
from jax.experimental import pallas as pl
from jax.experimental.pallas import tpu as pltpu
from jax.sharding import PartitionSpec as P

K = 9
RAD = 2
WIDTH = 2 * RAD + 1
TAPS = WIDTH * WIDTH
J = 32
EDGE = 8
PAD = 16
WIN = J + 2 * EDGE
SUB, LANES = 16, 128
MESH = pl.DeviceIdType.MESH


def kept_basis(basis, span_lo, span_hi):
    offsets = jnp.arange(TAPS, dtype=jnp.int32) // WIDTH - RAD
    keep = (offsets[None, :] >= span_lo[:, None]) & (offsets[None, :] <= span_hi[:, None])
    return jnp.where(keep[:, None, :], basis, jnp.zeros_like(basis))


def remote(src, dst, send, recv, device):
    copy = pltpu.make_async_remote_copy(
        src_ref=src, dst_ref=dst, send_sem=send, recv_sem=recv,
        device_id=device, device_id_type=MESH,
    )
    copy.start()
    return copy


def reduce_steps(
    lon, pairs, q, in_ref, out_ref, got_a, send_b, got_b, part, send_c, got_c,
    a_send, a_recv, b_send, b_recv, c_send, c_recv, d_send, d_recv, e_send, e_recv, f_send, f_recv,
):
    lat = lax.axis_index("lat")
    n = lax.axis_index("lon")
    core, z = lax.rem(lat, 2), lat // 2
    partner = (lat + 1 - 2 * core, n)
    piece = pairs * q
    half = lon * piece

    def lon_peer(s):
        return lax.rem(n + s, lon)

    def pair_peer(s):
        return lax.rem(z + s, pairs)

    theirs, mine = (1 - core) * half, core * half
    a_copies = []
    for s in range(lon):
        p = lon_peer(s + 1)
        a_copies.append(
            remote(
                in_ref.at[pl.ds(theirs + p * piece, piece)],
                got_a.at[pl.ds(p * piece, piece)],
                a_send.at[s], a_recv.at[s], partner,
            )
        )
    yield
    b_copies = []
    for s in range(lon):
        p = lon_peer(s + 1)
        a_copies[s].wait_recv()
        total = in_ref[pl.ds(mine + p * piece, piece)] + got_a[pl.ds(p * piece, piece)]
        if s < lon - 1:
            send_b[s] = total.astype(jnp.bfloat16)
            b_copies.append(remote(send_b.at[s], got_b.at[s], b_send.at[s], b_recv.at[s], (lat, p)))
        else:
            part[...] = total
    yield
    for s in range(lon - 1):
        b_copies[s].wait_recv()
        part[...] += got_b[s].astype(jnp.float32)
    c_copies = []
    for s in range(pairs - 1):
        p = pair_peer(s + 1)
        send_c[s] = part[pl.ds(p * q, q)].astype(jnp.bfloat16)
        c_copies.append(
            remote(send_c.at[s], got_c.at[s], c_send.at[s], c_recv.at[s], (p * 2 + core, n))
        )
    yield
    total = part[pl.ds(z * q, q)]
    for s in range(pairs - 1):
        c_copies[s].wait_recv()
        total = total + got_c[s].astype(jnp.float32)
    own = mine + n * piece
    out_ref[pl.ds(own + z * q, q)] = total.astype(jnp.bfloat16)

    d_copies, e_copies, f_copies = [], [], []

    def to_lon(t):
        src = out_ref.at[pl.ds(own + lax.rem(z + pairs - t, pairs) * q, q)]
        for s in range(lon - 1):
            e_copies.append(
                remote(src, src, e_send.at[t, s], e_recv.at[t, s], (lat, lon_peer(s + 1)))
            )

    def to_partner(s, p):
        src = out_ref.at[pl.ds(mine + p * piece, piece)]
        f_copies.append(remote(src, src, f_send.at[s], f_recv.at[s], partner))

    src = out_ref.at[pl.ds(own + z * q, q)]
    for s in range(pairs - 1):
        d_copies.append(
            remote(src, src, d_send.at[s], d_recv.at[s], (pair_peer(s + 1) * 2 + core, n))
        )
    to_lon(0)
    yield
    for t in range(1, pairs):
        d_copies[t - 1].wait_recv()
        to_lon(t)
    to_partner(0, n)
    yield
    for s in range(lon - 1):
        for t in range(pairs):
            e_copies[t * (lon - 1) + s].wait_recv()
        to_partner(s + 1, lax.rem(n + lon - s - 1, lon))
    for copy in f_copies:
        copy.wait_recv()
    for copy in a_copies + b_copies + c_copies + d_copies + e_copies + f_copies:
        copy.wait_send()


def halo_starts(src_ref, dst_ref, send, recv):
    rows, cols = src_ref.shape[0], src_ref.shape[1]
    lat, n = lax.axis_index("lat"), lax.axis_index("lon")
    lats, lons = lax.axis_size("lat"), lax.axis_size("lon")
    sides = {
        1: (pl.ds(rows - RAD, RAD), pl.ds(0, RAD)),
        0: (pl.ds(0, rows), pl.ds(RAD, rows)),
        -1: (pl.ds(0, RAD), pl.ds(RAD + rows, RAD)),
    }
    spans = {
        1: (pl.ds(cols - PAD, PAD), pl.ds(0, PAD)),
        0: (pl.ds(0, cols), pl.ds(PAD, cols)),
        -1: (pl.ds(0, PAD), pl.ds(PAD + cols, PAD)),
    }
    present = {1: lat < lats - 1, -1: lat > 0}
    copies = {1: [], 0: [], -1: []}
    for dy in (1, -1, 0):
        for dx in (0, 1, -1):
            if dy == 0 and dx == 0:
                continue
            slot = (dy + 1) * 3 + dx + 1
            copies[dy].append(
                pltpu.make_async_remote_copy(
                    src_ref=src_ref.at[sides[dy][0], spans[dx][0]],
                    dst_ref=dst_ref.at[sides[dy][1], spans[dx][1]],
                    send_sem=send.at[slot], recv_sem=recv.at[slot],
                    device_id=(lat + dy, lax.rem(n + dx + lons, lons)), device_id_type=MESH,
                )
            )
    for dy in (1, -1):
        @pl.when(present[dy])
        def _():
            for copy in copies[dy]:
                copy.start()
    for copy in copies[0]:
        copy.start()

    def received():
        for copy in copies[0]:
            copy.wait_recv()
        for dy in (1, -1):
            @pl.when(present[-dy])
            def _():
                for copy in copies[dy]:
                    copy.wait_recv()

    def sent():
        for copy in copies[0]:
            copy.wait_send()
        for dy in (1, -1):
            @pl.when(present[dy])
            def _():
                for copy in copies[dy]:
                    copy.wait_send()

    return received, sent


def kernel(
    scale, tile, lon, pairs, q, f_ref, c_ref, b_ref, w_hbm, mixed_ref, gi_ref, gw_ref,
    fx, cx, bx, w_ref, wt_ref, v_ref, u_ref, fa_ref, ca_ref, y_ref, acc_ref, groups_ref,
    local_sem, f_send, f_recv, c_send, c_recv, b_send, b_recv, *reduce_scratch,
):
    rows, lon_count, channels = f_ref.shape
    tiles = lon_count // tile
    lat, n = lax.axis_index("lat"), lax.axis_index("lon")
    lats = lax.axis_size("lat")
    core, z = lax.rem(lat, 2), lat // 2
    has = {1: lat < lats - 1, -1: lat > 0}

    barrier = pltpu.get_barrier_semaphore()
    for dy in (1, -1):
        @pl.when(has[dy])
        def _():
            for dx in (-1, 0, 1):
                there = (lat + dy, lax.rem(n + dx + lon, lon))
                pl.semaphore_signal(barrier, inc=1, device_id=there, device_id_type=MESH)
    for s in range(1, lon):
        there = (lat, lax.rem(n + s, lon))
        pl.semaphore_signal(barrier, inc=1, device_id=there, device_id_type=MESH)
    for s in range(1, pairs):
        there = (lax.rem(z + s, pairs) * 2 + core, n)
        pl.semaphore_signal(barrier, inc=1, device_id=there, device_id_type=MESH)
    here = pl.ds(RAD, rows)
    middle = pl.ds(PAD, lon_count)
    locals_ = [
        pltpu.make_async_copy(f_ref, fx.at[here, middle], local_sem.at[0]),
        pltpu.make_async_copy(c_ref, cx.at[here, middle], local_sem.at[1]),
        pltpu.make_async_copy(w_hbm, w_ref, local_sem.at[2]),
    ]
    for copy in locals_:
        copy.start()
    bx[here] = b_ref[...]
    for dy, edge in ((1, 0), (-1, RAD + rows)):
        @pl.when(jnp.logical_not(has[-dy]))
        def _():
            fx[edge : edge + RAD] = jnp.zeros((RAD,) + fx.shape[1:], jnp.bfloat16)
            cx[edge : edge + RAD] = jnp.zeros((RAD,) + cx.shape[1:], jnp.bfloat16)
            bx[edge : edge + RAD] = jnp.zeros((RAD,) + bx.shape[1:], jnp.float32)
    pl.semaphore_wait(
        barrier,
        3 * has[1].astype(jnp.int32) + 3 * has[-1].astype(jnp.int32) + lon - 1 + pairs - 1,
    )

    b_copies = {}
    for slot, dy, src, dst in ((0, 1, rows - RAD, 0), (1, -1, 0, RAD + rows)):
        b_copies[dy] = pltpu.make_async_remote_copy(
            src_ref=b_ref.at[pl.ds(src, RAD)], dst_ref=bx.at[pl.ds(dst, RAD)],
            send_sem=b_send.at[slot], recv_sem=b_recv.at[slot],
            device_id=(lat + dy, n), device_id_type=MESH,
        )

        @pl.when(has[dy])
        def _():
            b_copies[dy].start()
    f_received, f_sent = halo_starts(f_ref, fx, f_send, f_recv)
    c_received, c_sent = halo_starts(c_ref, cx, c_send, c_recv)

    locals_[2].wait()
    for k in range(K):
        block = slice(k * channels, (k + 1) * channels)
        wt_ref[block] = w_ref[block].T

    for dy in (1, -1):
        @pl.when(has[-dy])
        def _():
            b_copies[dy].wait_recv()
    taps = lax.broadcasted_iota(jnp.int32, (LANES, 256), 0)
    lane = lax.broadcasted_iota(jnp.int32, (LANES, 256), 1)

    def segment(lanes):
        return sum((lanes >= m * WIN).astype(jnp.int32) for m in range(1, WIDTH))

    seg = segment(lane)
    coef = bx[...].astype(jnp.bfloat16).reshape((rows + 2 * RAD) * SUB, LANES)

    def pick(want):
        chosen = jnp.where(taps == want, 1.0, 0.0).astype(jnp.bfloat16)
        out = jnp.dot(coef, chosen, preferred_element_type=jnp.float32)
        return out.reshape(rows + 2 * RAD, SUB, 256)

    for e in range(WIDTH):
        v_ref[e] = pick(seg * WIDTH + e)
        u_ref[e] = pick((WIDTH - 1 - seg) * WIDTH + WIDTH - 1 - e)
    lane = lax.broadcasted_iota(jnp.int32, (J, 256), 1)
    seg_j = segment(lane)
    col = lane - seg_j * WIN - lax.broadcasted_iota(jnp.int32, (J, 256), 0) - (EDGE - RAD)
    seg_k = segment(lax.broadcasted_iota(jnp.int32, (SUB, 256), 1))

    def build(i, carry):
        adjoint = []
        for e in range(WIDTH):
            line = u_ref[e, i]
            for r in range(1, WIDTH):
                line = jnp.where(seg_k == r, u_ref[e, i + r], line)
            adjoint.append(line)
        forward = [v_ref[e, i + RAD] for e in range(WIDTH)]
        for lines, a_ref in ((forward, fa_ref), (adjoint, ca_ref)):
            for k in range(K):
                a = jnp.zeros((J, 256), jnp.float32)
                for e in range(WIDTH):
                    a = jnp.where(col == e, jnp.broadcast_to(lines[e][k : k + 1], (J, 256)), a)
                a_ref[i, k * J : (k + 1) * J] = a.astype(jnp.bfloat16)
        return carry

    lax.fori_loop(0, rows, build, 0)
    acc_ref[...] = jnp.zeros_like(acc_ref)

    def stencil(x_ref, a_ref, i, start):
        a = a_ref[i][:, : WIDTH * WIN]
        for b in range(tile // J):
            first = pl.multiple_of(start + b * J, PAD)
            x = x_ref[pl.ds(i, WIDTH), pl.ds(first, J + 2 * PAD), :]
            x = x[:, PAD - EDGE : PAD - EDGE + WIN].reshape(WIDTH * WIN, channels)
            y = jnp.dot(a, x, preferred_element_type=jnp.float32).astype(jnp.bfloat16)
            for k in range(K):
                y_ref[b * J : (b + 1) * J, k * channels : (k + 1) * channels] = y[k * J : (k + 1) * J]

    def forward_step(s, carry):
        i = s // tiles
        start = pl.multiple_of((s % tiles) * tile, tile)
        stencil(fx, fa_ref, i, start)
        mixed_ref[i, pl.ds(start, tile), :] = jnp.dot(
            y_ref[...], w_ref[...], preferred_element_type=jnp.float32
        ).astype(jnp.bfloat16)
        cot = cx[i + RAD, pl.ds(pl.multiple_of(start + PAD, PAD), tile), :]
        acc_ref[...] += jnp.dot(cot.T, y_ref[...], preferred_element_type=jnp.float32)
        return carry

    def adjoint_step(s, carry):
        i = s // tiles
        start = pl.multiple_of((s % tiles) * tile, tile)
        stencil(cx, ca_ref, i, start)
        gi_ref[i, pl.ds(start, tile), :] = jnp.dot(
            y_ref[...], wt_ref[...], preferred_element_type=jnp.float32
        ).astype(jnp.bfloat16)
        return carry

    locals_[0].wait()
    locals_[1].wait()
    f_received()
    lax.fori_loop(0, rows * tiles, forward_step, 0)
    per = channels // SUB
    for k in range(K):
        turned = acc_ref[:, k * channels : (k + 1) * channels].T * scale
        for h in range(channels // LANES):
            first = (k * (channels // LANES) + h) * per
            block = turned[:, h * LANES : (h + 1) * LANES]
            groups_ref[first : first + per] = block.reshape(per, SUB, LANES)
    used = K * per * (channels // LANES)
    if groups_ref.shape[0] > used:
        groups_ref[used:] = jnp.zeros((groups_ref.shape[0] - used, SUB, LANES), jnp.float32)

    reduction = reduce_steps(lon, pairs, q, groups_ref, gw_ref, *reduce_scratch)
    next(reduction)
    c_received()
    steps = rows * tiles
    cuts = [0, max(1, steps // 4), max(1, steps * 3 // 4), steps]
    for lo, hi in zip(cuts[:-1], cuts[1:]):
        lax.fori_loop(lo, hi, adjoint_step, 0)
        next(reduction)
    for _ in reduction:
        pass
    f_sent()
    c_sent()
    for dy in (1, -1):
        @pl.when(has[dy])
        def _():
            b_copies[dy].wait_send()


def per_device(features, basis, span_lo, span_hi, weight, cotangent):
    rows, lon_count, channels = features.shape
    kept = kept_basis(basis, span_lo, span_hi)
    coef = jnp.pad(kept, ((0, 0), (0, SUB - K), (0, LANES - TAPS)))
    scale = 1.0 / math.sqrt(rows * lax.axis_size("lat") * lon_count * lax.axis_size("lon"))
    tile = 512
    lon, pairs = lax.axis_size("lon"), lax.axis_size("lat") // 2
    used = weight.size // (SUB * LANES)
    q = -(-used // (2 * lon * pairs))
    piece = pairs * q
    groups = 2 * lon * piece
    dma = pltpu.SemaphoreType.DMA
    bf16, f32 = jnp.bfloat16, jnp.float32
    vmem = pl.BlockSpec(memory_space=pltpu.VMEM)
    anywhere = pl.BlockSpec(memory_space=pl.ANY)
    wide = (rows + 2 * RAD, lon_count + 2 * PAD, channels)
    mixed, grad_input, total = pl.pallas_call(
        functools.partial(kernel, scale, tile, lon, pairs, q),
        out_shape=(
            jax.ShapeDtypeStruct(features.shape, bf16),
            jax.ShapeDtypeStruct(features.shape, bf16),
            jax.ShapeDtypeStruct((groups, SUB, LANES), bf16),
        ),
        in_specs=[anywhere, anywhere, vmem, anywhere],
        out_specs=[vmem] * 3,
        scratch_shapes=[
            pltpu.VMEM(wide, bf16),
            pltpu.VMEM(wide, bf16),
            pltpu.VMEM((rows + 2 * RAD, SUB, LANES), f32),
            pltpu.VMEM((K * channels, channels), bf16),
            pltpu.VMEM((K * channels, channels), bf16),
            pltpu.VMEM((WIDTH, rows + 2 * RAD, SUB, 256), f32),
            pltpu.VMEM((WIDTH, rows + 2 * RAD, SUB, 256), f32),
            pltpu.VMEM((rows, K * J, 256), bf16),
            pltpu.VMEM((rows, K * J, 256), bf16),
            pltpu.VMEM((tile, K * channels), bf16),
            pltpu.VMEM((channels, K * channels), f32),
            pltpu.VMEM((groups, SUB, LANES), f32),
            dma((3,)), dma((9,)), dma((9,)), dma((9,)), dma((9,)), dma((2,)), dma((2,)),
            pltpu.VMEM((lon * piece, SUB, LANES), f32),
            pltpu.VMEM((lon - 1, piece, SUB, LANES), bf16),
            pltpu.VMEM((lon - 1, piece, SUB, LANES), bf16),
            pltpu.VMEM((piece, SUB, LANES), f32),
            pltpu.VMEM((pairs - 1, q, SUB, LANES), bf16),
            pltpu.VMEM((pairs - 1, q, SUB, LANES), bf16),
            dma((lon,)), dma((lon,)),
            dma((lon - 1,)), dma((lon - 1,)),
            dma((pairs - 1,)), dma((pairs - 1,)),
            dma((pairs - 1,)), dma((pairs - 1,)),
            dma((pairs, lon - 1)), dma((pairs, lon - 1)),
            dma((lon,)), dma((lon,)),
        ],
        compiler_params=pltpu.CompilerParams(
            collective_id=0, has_side_effects=True, vmem_limit_bytes=50 * 2**20
        ),
    )(features, cotangent, coef, weight.reshape(K * channels, channels))
    total = total[:used].astype(f32).reshape(K, channels // LANES, channels, LANES)
    grad_weight = jnp.swapaxes(total, 1, 2).reshape(weight.shape)
    return (mixed, grad_input, grad_weight)


def solution(mesh):
    return jax.shard_map(
        per_device,
        mesh=mesh,
        in_specs=(
            P("lat", "lon", None),
            P("lat", None, None),
            P("lat"),
            P("lat"),
            P(),
            P("lat", "lon", None),
        ),
        out_specs=(P("lat", "lon", None), P("lat", "lon", None), P()),
        check_vma=False,
    )
```

time: 103 us -> 59.3 us (0.58)
  starting transfers between devices: 21.9 us -> 0 us
  local copies, waits for them, and re-layouts: 16.3 us -> 3.17 us
  other arithmetic: 10.9 us -> 4.38 us
  waiting for transfers between devices: 3.52 us -> 0 us
  Pallas kernels: 49.1 us -> 50.8 us
    ppermute x10 -> x0, starting transfers between devices: 21.9 us -> none  [passed(): return lax.ppermute(block, axis, route)]
    concatenate x3 -> x0, other arithmetic: 5.75 us -> none  [the longest x2 5.72 us: extended(): return jnp.concatenate([above, block, below], axis=0)]
    slice x6 -> x0, local copies, waits for them, and re-layouts: 4.82 us -> none  [the longest x2 2.69 us: extended(): high = passed(block[:, :EDGE], 'lon', -1, True)]
    broadcast_in_dim x19 -> x0, local copies, waits for them, and re-layouts: 4.18 us -> none  [the longest x17 2.93 us: banded(): out = jnp.where((where_col == e)[None, None], spread[:, :, None, :, e], out)]
    ppermute x10 -> x0, waiting for transfers between devices: 3.52 us -> none  [passed(): return lax.ppermute(block, axis, route)]
    pallas_call x2 -> x1, Pallas kernels: 49.1 us -> 50.8 us  [per_device(): pl.pallas_call(functools.partial(kernel, scale, tile, lon, pairs, q), out...]
    transpose x1 -> x0, local copies, waits for them, and re-layouts: 1.54 us -> none  [per_device(): wt = jnp.swapaxes(weight, 1, 2).reshape(K * channels, channels)]
    reshape x2 -> x0, local copies, waits for them, and re-layouts: 1.43 us -> none  [banded(): spread = jnp.repeat(coef.astype(jnp.bfloat16), WIN, axis=2)]
  transfers between devices with their start and end apart: 10 -> 0, of which waited for: 1 -> 0; matrix products, arithmetic and copies ran while one was open for 18% -> 0% of each run, Pallas kernels for 0% -> 0%
where the time goes in v3:
time: 59.3 us; the launch traced here: 59 us
  Pallas kernels  50.8 us (86%)
  other arithmetic  4.38 us (7%)
  local copies, waits for them, and re-layouts  3.17 us (5%)
  between operations  0.65 us (1%)
    pallas_call x1, Pallas kernels, per_device(): pl.pallas_call(functools.partial(kernel, scale, tile, lon, pairs, q), out...  50.8 us
    unnamed x4, local copies, waits for them, and re-layouts  3.16 us
    reshape x1, other arithmetic, per_device(): grad_weight = jnp.swapaxes(total, 1, 2).reshape(weight.shape)  2.89 us

profile of v3, /device:TPU:0, one launch (start us, length us, event | category | flops | bytes accessed | tf_op | source)
XLA Modules:
  0.0 59.0 jit_solution(18089612039428544366)
XLA Ops:
  0.6 0.7 %compare_and_fusion = pred[4,25]{1,0:T(4,128)(4,1)S(1)} fusion(s32[25]{0:T(128)S(1)} %fusion, s32[4]{0:T(128)} %param.9, s32[4]{0:T(128)} %param.8), kind=kLoop, calls=%fused_computation.3 | loop fusion | flops 300 | bytes 232 | tf_op jit(solution)/shard_map/and | solution.py:25
  1.4 0.7 %copy_select_fusion = f32[4,9,25]{2,1,0:T(8,128)S(1)} fusion(f32[4,9,25]{2,0,1:T(4,128)} %param.7, pred[4,25]{1,0:T(4,128)(4,1)S(1)} %compare_and_fusion), kind=kLoop, calls=%fused_computation.2 | loop fusion | flops 900 | bytes 7300 | tf_op jit(solution)/shard_map/jit(_where)/select_n | solution.py:26
  2.1 0.0 copy-start
  2.1 1.2 %copy-done = bf16[4,512,256]{2,1,0:T(8,128)(2,1)S(1)} copy-done((bf16[4,512,256]{2,1,0:T(8,128)(2,1)S(1)}, bf16[4,512,256]{2,1,0:T(8,128)(2,1)}, u32[]{:S(2)}) %copy-start) | copy-done | bytes 1048600
  3.4 50.8 %shard_map.85 = (bf16[4,512,256]{2,1,0:T(8,128)(2,1)S(1)}, bf16[4,512,256]{2,1,0:T(8,128)(2,1)S(1)}, bf16[288,16,128]{2,1,0:T(8,128)(2,1)}) custom-call(bf16[4,512,256]{2,1,0:T(8,128)(2,1)S(1)} %copy-done, bf16[4,512,256]{2,1,0:T(8,128)(2,1)} %c_ref.1, f32[4,16,128]{2,1,0:T(8,128)S(1)} %pad.4.b_ref, bf16[2304,256]{1,0:T(8,128)(2,1)} %bitcast.9), custom_call_target="tpu_custom_call" | custom-call | tf_op jit(solution)/shard_map/pallas_call | solution.py:378
  54.2 2.9 %copy_bitcast_fusion = f32[9,256,256]{2,1,0:T(8,128)} fusion(bf16[9,2,256,128]{3,2,1,0:T(8,128)(2,1)} %bitcast.10), kind=kLoop, calls=%fused_computation | loop fusion | flops 589824 | bytes 3538944 | tf_op jit(solution)/shard_map/reshape | solution.py:419
  57.1 1.0 %copy.16 = bf16[4,512,256]{2,1,0:T(8,128)(2,1)} copy(bf16[4,512,256]{2,1,0:T(8,128)(2,1)S(1)} %get-tuple-element.12) | data formatting | bytes 2097152
  58.1 1.0 %copy.17 = bf16[4,512,256]{2,1,0:T(8,128)(2,1)} copy(bf16[4,512,256]{2,1,0:T(8,128)(2,1)S(1)} %get-tuple-element.13) | data formatting | bytes 2097152
  (2 shorter events, 0.0 us)
Async XLA Ops:
  2.1 1.2 %copy-start = (bf16[4,512,256]{2,1,0:T(8,128)(2,1)S(1)}, bf16[4,512,256]{2,1,0:T(8,128)(2,1)}, u32[]{:S(2)}) copy-start(bf16[4,512,256]{2,1,0:T(8,128)(2,1)} %f_ref.1) | copy-start | bytes 3145732

commit v4 on v3

v4 whole, which is shorter than its diff:
```python
import functools
import math

import jax
import jax.numpy as jnp
from jax import lax
from jax.experimental import pallas as pl
from jax.experimental.pallas import tpu as pltpu
from jax.sharding import PartitionSpec as P

K = 9
RAD = 2
WIDTH = 2 * RAD + 1
TAPS = WIDTH * WIDTH
J = 32
EDGE = 8
PAD = 16
WIN = J + 2 * EDGE
SUB, LANES = 16, 128
MESH = pl.DeviceIdType.MESH


def remote(src, dst, send, recv, device):
    copy = pltpu.make_async_remote_copy(
        src_ref=src, dst_ref=dst, send_sem=send, recv_sem=recv,
        device_id=device, device_id_type=MESH,
    )
    copy.start()
    return copy


def reduce_steps(
    lon, pairs, q, in_ref, out_ref, got_a, send_b, got_b, part, send_c, got_c,
    a_send, a_recv, b_send, b_recv, c_send, c_recv, d_send, d_recv, e_send, e_recv, f_send, f_recv,
):
    lat = lax.axis_index("lat")
    n = lax.axis_index("lon")
    core, z = lax.rem(lat, 2), lat // 2
    partner = (lat + 1 - 2 * core, n)
    piece = pairs * q
    half = lon * piece

    def lon_peer(s):
        return lax.rem(n + s, lon)

    def pair_peer(s):
        return lax.rem(z + s, pairs)

    theirs, mine = (1 - core) * half, core * half
    a_copies = []
    for s in range(lon):
        p = lon_peer(s + 1)
        a_copies.append(
            remote(
                in_ref.at[pl.ds(theirs + p * piece, piece)],
                got_a.at[pl.ds(p * piece, piece)],
                a_send.at[s], a_recv.at[s], partner,
            )
        )
    yield
    b_copies = []
    for s in range(lon):
        p = lon_peer(s + 1)
        a_copies[s].wait_recv()
        total = in_ref[pl.ds(mine + p * piece, piece)] + got_a[pl.ds(p * piece, piece)]
        if s < lon - 1:
            send_b[s] = total.astype(jnp.bfloat16)
            b_copies.append(remote(send_b.at[s], got_b.at[s], b_send.at[s], b_recv.at[s], (lat, p)))
        else:
            part[...] = total
    yield
    for s in range(lon - 1):
        b_copies[s].wait_recv()
        part[...] += got_b[s].astype(jnp.float32)
    c_copies = []
    for s in range(pairs - 1):
        p = pair_peer(s + 1)
        send_c[s] = part[pl.ds(p * q, q)].astype(jnp.bfloat16)
        c_copies.append(
            remote(send_c.at[s], got_c.at[s], c_send.at[s], c_recv.at[s], (p * 2 + core, n))
        )
    yield
    total = part[pl.ds(z * q, q)]
    for s in range(pairs - 1):
        c_copies[s].wait_recv()
        total = total + got_c[s].astype(jnp.float32)
    own = mine + n * piece
    out_ref[pl.ds(own + z * q, q)] = total.astype(jnp.bfloat16)

    d_copies, e_copies, f_copies = [], [], []

    def to_lon(t):
        src = out_ref.at[pl.ds(own + lax.rem(z + pairs - t, pairs) * q, q)]
        for s in range(lon - 1):
            e_copies.append(
                remote(src, src, e_send.at[t, s], e_recv.at[t, s], (lat, lon_peer(s + 1)))
            )

    def to_partner(s, p):
        src = out_ref.at[pl.ds(mine + p * piece, piece)]
        f_copies.append(remote(src, src, f_send.at[s], f_recv.at[s], partner))

    src = out_ref.at[pl.ds(own + z * q, q)]
    for s in range(pairs - 1):
        d_copies.append(
            remote(src, src, d_send.at[s], d_recv.at[s], (pair_peer(s + 1) * 2 + core, n))
        )
    to_lon(0)
    yield
    for t in range(1, pairs):
        d_copies[t - 1].wait_recv()
        to_lon(t)
    to_partner(0, n)
    yield
    for s in range(lon - 1):
        for t in range(pairs):
            e_copies[t * (lon - 1) + s].wait_recv()
        to_partner(s + 1, lax.rem(n + lon - s - 1, lon))
    yield
    for copy in f_copies:
        copy.wait_recv()
    for copy in a_copies + b_copies + c_copies + d_copies + e_copies + f_copies:
        copy.wait_send()


def halo_starts(src_ref, dst_ref, send, recv):
    rows, cols = src_ref.shape[0], src_ref.shape[1]
    lat, n = lax.axis_index("lat"), lax.axis_index("lon")
    lats, lons = lax.axis_size("lat"), lax.axis_size("lon")
    sides = {
        1: (pl.ds(rows - RAD, RAD), pl.ds(0, RAD)),
        0: (pl.ds(0, rows), pl.ds(RAD, rows)),
        -1: (pl.ds(0, RAD), pl.ds(RAD + rows, RAD)),
    }
    spans = {
        1: (pl.ds(cols - PAD, PAD), pl.ds(0, PAD)),
        0: (pl.ds(0, cols), pl.ds(PAD, cols)),
        -1: (pl.ds(0, PAD), pl.ds(PAD + cols, PAD)),
    }
    present = {1: lat < lats - 1, -1: lat > 0}
    copies = {1: [], 0: [], -1: []}
    for dy in (1, -1, 0):
        for dx in (0, 1, -1):
            if dy == 0 and dx == 0:
                continue
            slot = (dy + 1) * 3 + dx + 1
            copies[dy].append(
                pltpu.make_async_remote_copy(
                    src_ref=src_ref.at[sides[dy][0], spans[dx][0]],
                    dst_ref=dst_ref.at[sides[dy][1], spans[dx][1]],
                    send_sem=send.at[slot], recv_sem=recv.at[slot],
                    device_id=(lat + dy, lax.rem(n + dx + lons, lons)), device_id_type=MESH,
                )
            )
    for dy in (1, -1):
        @pl.when(present[dy])
        def _():
            for copy in copies[dy]:
                copy.start()
    for copy in copies[0]:
        copy.start()

    core = lax.rem(lat, 2)

    def wait(side, condition):
        @pl.when(condition)
        def _():
            for copy in copies[side]:
                copy.wait_recv()

    def near():
        for copy in copies[0]:
            copy.wait_recv()
        wait(-1, core == 0)
        wait(1, core == 1)

    def far():
        wait(1, (core == 0) & present[-1])
        wait(-1, (core == 1) & present[1])

    def sent():
        for copy in copies[0]:
            copy.wait_send()
        for dy in (1, -1):
            @pl.when(present[dy])
            def _():
                for copy in copies[dy]:
                    copy.wait_send()

    return near, far, sent


def kernel(
    scale, lon, pairs, q, f_ref, c_ref, basis_ref, lo_ref, hi_ref, w_hbm, mixed_hbm, gi_hbm, gw_ref,
    fx, cx, bx, w_ref, wt_ref, v_ref, u_ref, fa_ref, ca_ref, y_ref, ct_ref, mixed_ref, gi_ref,
    groups_ref, sums_ref, local_sem, f_send, f_recv, c_send, c_recv, b_send, b_recv, *reduce_scratch,
):
    rows, lon_count, channels = f_ref.shape
    lat, n = lax.axis_index("lat"), lax.axis_index("lon")
    lats = lax.axis_size("lat")
    core, z = lax.rem(lat, 2), lat // 2
    has = {1: lat < lats - 1, -1: lat > 0}

    barrier = pltpu.get_barrier_semaphore()
    for dy in (1, -1):
        @pl.when(has[dy])
        def _():
            for dx in (-1, 0, 1):
                there = (lat + dy, lax.rem(n + dx + lon, lon))
                pl.semaphore_signal(barrier, inc=1, device_id=there, device_id_type=MESH)
    for s in range(1, lon):
        there = (lat, lax.rem(n + s, lon))
        pl.semaphore_signal(barrier, inc=1, device_id=there, device_id_type=MESH)
    for s in range(1, pairs):
        there = (lax.rem(z + s, pairs) * 2 + core, n)
        pl.semaphore_signal(barrier, inc=1, device_id=there, device_id_type=MESH)
    here = pl.ds(RAD, rows)
    middle = pl.ds(PAD, lon_count)
    locals_ = [
        pltpu.make_async_copy(f_ref, fx.at[here, middle], local_sem.at[0]),
        pltpu.make_async_copy(c_ref, cx.at[here, middle], local_sem.at[1]),
        pltpu.make_async_copy(w_hbm, w_ref, local_sem.at[2]),
    ]
    for copy in locals_:
        copy.start()
    offset = lax.broadcasted_iota(jnp.int32, (K, TAPS), 1)
    offset = sum((offset >= m * WIDTH).astype(jnp.int32) for m in range(1, WIDTH)) - RAD
    bx[here] = jnp.zeros((rows,) + bx.shape[1:], jnp.float32)
    for i in range(rows):
        keep = (offset >= lo_ref[i]) & (offset <= hi_ref[i])
        bx[RAD + i, 0:K, 0:TAPS] = jnp.where(keep, basis_ref[i], 0.0)
    for dy, edge in ((1, 0), (-1, RAD + rows)):
        @pl.when(jnp.logical_not(has[-dy]))
        def _():
            fx[edge : edge + RAD] = jnp.zeros((RAD,) + fx.shape[1:], jnp.bfloat16)
            cx[edge : edge + RAD] = jnp.zeros((RAD,) + cx.shape[1:], jnp.bfloat16)
            bx[edge : edge + RAD] = jnp.zeros((RAD,) + bx.shape[1:], jnp.float32)
    pl.semaphore_wait(
        barrier,
        3 * has[1].astype(jnp.int32) + 3 * has[-1].astype(jnp.int32) + lon - 1 + pairs - 1,
    )

    f_near, f_far, f_sent = halo_starts(f_ref, fx, f_send, f_recv)
    b_copies = {}
    for slot, dy, src, dst in ((0, 1, rows, 0), (1, -1, RAD, RAD + rows)):
        b_copies[dy] = pltpu.make_async_remote_copy(
            src_ref=bx.at[pl.ds(src, RAD)], dst_ref=bx.at[pl.ds(dst, RAD)],
            send_sem=b_send.at[slot], recv_sem=b_recv.at[slot],
            device_id=(lat + dy, n), device_id_type=MESH,
        )

        @pl.when(has[dy])
        def _():
            b_copies[dy].start()

    taps = lax.broadcasted_iota(jnp.int32, (LANES, 256), 0)

    def segment(shape):
        lanes = lax.broadcasted_iota(jnp.int32, shape, 1)
        return sum((lanes >= m * WIN).astype(jnp.int32) for m in range(1, WIDTH))

    def pick(coef, want):
        chosen = jnp.where(taps == want, 1.0, 0.0).astype(jnp.bfloat16)
        out = jnp.dot(coef, chosen, preferred_element_type=jnp.float32)
        return out.reshape(coef.shape[0] // SUB, SUB, 256)

    def place(lines, a_ref, i):
        lane = lax.broadcasted_iota(jnp.int32, (J, 256), 1)
        row = lax.broadcasted_iota(jnp.int32, (J, 256), 0)
        col = lane - segment((J, 256)) * WIN - row - (EDGE - RAD)
        for k in range(K):
            a = jnp.zeros((J, 256), jnp.float32)
            for e in range(WIDTH):
                a = jnp.where(col == e, jnp.broadcast_to(lines[e][k : k + 1], (J, 256)), a)
            a_ref[i, k * J : (k + 1) * J] = a.astype(jnp.bfloat16)

    def build_forward():
        coef = bx[here].astype(jnp.bfloat16).reshape(rows * SUB, LANES)
        seg = segment((LANES, 256))
        for e in range(WIDTH):
            v_ref[e] = pick(coef, seg * WIDTH + e)

        def build(i, carry):
            place([v_ref[e, i] for e in range(WIDTH)], fa_ref, i)
            return carry

        lax.fori_loop(0, rows, build, 0)

    def build_adjoint():
        for dy in (1, -1):
            @pl.when(has[-dy])
            def _():
                b_copies[dy].wait_recv()
        coef = bx[...].astype(jnp.bfloat16).reshape((rows + 2 * RAD) * SUB, LANES)
        seg = segment((LANES, 256))
        for e in range(WIDTH):
            u_ref[e] = pick(coef, (WIDTH - 1 - seg) * WIDTH + WIDTH - 1 - e)
        seg = segment((SUB, 256))

        def build(i, carry):
            lines = []
            for e in range(WIDTH):
                line = u_ref[e, i]
                for r in range(1, WIDTH):
                    line = jnp.where(seg == r, u_ref[e, i + r], line)
                lines.append(line)
            place(lines, ca_ref, i)
            return carry

        lax.fori_loop(0, rows, build, 0)

    def stencil(x_ref, a_ref, i):
        a = a_ref[i][:, : WIDTH * WIN]
        for b in range(lon_count // J):
            x = x_ref[pl.ds(i, WIDTH), b * J : b * J + J + 2 * PAD, :]
            x = x[:, PAD - EDGE : PAD - EDGE + WIN].reshape(WIDTH * WIN, channels)
            y = jnp.dot(a, x, preferred_element_type=jnp.float32).astype(jnp.bfloat16)
            for k in range(K):
                y_ref[i, b * J : (b + 1) * J, k * channels : (k + 1) * channels] = y[k * J : (k + 1) * J]

    def mix(i, weights, out_ref):
        out_ref[i] = jnp.dot(
            y_ref[i], weights[...], preferred_element_type=jnp.float32
        ).astype(jnp.bfloat16)

    def looped(lo, hi, step):
        def body(i, carry):
            step(i)
            return carry

        lax.fori_loop(lo, hi, body, 0)

    halfway = rows // 2
    first_near = halfway * (1 - core)
    first_far = halfway * core
    build_forward()
    locals_[0].wait()
    f_near()
    looped(first_near, first_near + halfway, lambda i: stencil(fx, fa_ref, i))
    locals_[1].wait()
    for i in range(rows):
        ct_ref[:, i * lon_count : (i + 1) * lon_count] = cx[RAD + i, PAD : PAD + lon_count].T
    locals_[2].wait()
    looped(first_near, first_near + halfway, lambda i: mix(i, w_ref, mixed_ref))
    f_far()
    c_near, c_far, c_sent = halo_starts(c_ref, cx, c_send, c_recv)
    looped(first_far, first_far + halfway, lambda i: stencil(fx, fa_ref, i))

    chunks = groups_ref.shape[0]
    each = K // chunks
    per = channels // SUB
    halves = channels // LANES
    used = each * halves * per

    def product(m):
        for j in range(each):
            k = m * each + j
            total = jnp.zeros((channels, channels), jnp.float32)
            for i in range(rows):
                total += jnp.dot(
                    ct_ref[:, i * lon_count : (i + 1) * lon_count],
                    y_ref[i, :, k * channels : (k + 1) * channels],
                    preferred_element_type=jnp.float32,
                )
            turned = total.T * scale
            for h in range(halves):
                at = (j * halves + h) * per
                block = turned[:, h * LANES : (h + 1) * LANES]
                groups_ref[m, at : at + per] = block.reshape(per, SUB, LANES)
        rest = groups_ref.shape[1] - used
        if rest:
            groups_ref[m, used:] = jnp.zeros((rest, SUB, LANES), jnp.float32)

    def unpack(m):
        for j in range(each):
            k = m * each + j
            for h in range(halves):
                at = (j * halves + h) * per
                gw_ref[k * channels : (k + 1) * channels, h * LANES : (h + 1) * LANES] = sums_ref[
                    m, at : at + per
                ].reshape(channels, LANES)

    def reduction(m):
        scratch = [ref.at[m] for ref in reduce_scratch]
        yield from reduce_steps(lon, pairs, q, groups_ref.at[m], sums_ref.at[m], *scratch)
        unpack(m)

    sums = [reduction(m) for m in range(chunks)]

    def go(*which):
        for m in which:
            next(sums[m], None)

    out_copies = [
        pltpu.make_async_copy(mixed_ref, mixed_hbm, local_sem.at[3]),
        pltpu.make_async_copy(gi_ref, gi_hbm, local_sem.at[4]),
    ]

    def adjoint(i):
        stencil(cx, ca_ref, i)
        mix(i, wt_ref, gi_ref)

    product(0)
    go(0)
    product(1)
    go(1, 0)
    product(2)
    go(2, 1)
    looped(first_far, first_far + 1, lambda i: mix(i, w_ref, mixed_ref))
    go(2, 0)
    looped(first_far + 1, first_far + halfway, lambda i: mix(i, w_ref, mixed_ref))
    out_copies[0].start()
    go(1, 0)
    for k in range(K):
        block = slice(k * channels, (k + 1) * channels)
        wt_ref[block] = w_ref[block].T
    build_adjoint()
    go(2, 1, 0)
    c_near()
    looped(first_near, first_near + 1, adjoint)
    go(2, 1, 0)
    looped(first_near + 1, first_near + halfway, adjoint)
    go(2, 1, 0)
    c_far()
    looped(first_far, first_far + 1, adjoint)
    go(2, 1)
    looped(first_far + 1, first_far + halfway, adjoint)
    out_copies[1].start()
    for one in sums:
        for _ in one:
            pass
    f_sent()
    c_sent()
    for dy in (1, -1):
        @pl.when(has[dy])
        def _():
            b_copies[dy].wait_send()
    for copy in out_copies:
        copy.wait()


def per_device(features, basis, span_lo, span_hi, weight, cotangent):
    rows, lon_count, channels = features.shape
    scale = 1.0 / math.sqrt(rows * lax.axis_size("lat") * lon_count * lax.axis_size("lon"))
    lon, pairs = lax.axis_size("lon"), lax.axis_size("lat") // 2
    chunks = 3
    q = -(-weight.size // (SUB * LANES * chunks * 2 * lon * pairs))
    piece = pairs * q
    groups = 2 * lon * piece
    bf16, f32 = jnp.bfloat16, jnp.float32
    vmem = pl.BlockSpec(memory_space=pltpu.VMEM)
    smem = pl.BlockSpec(memory_space=pltpu.SMEM)
    anywhere = pl.BlockSpec(memory_space=pl.ANY)
    wide = (rows + 2 * RAD, lon_count + 2 * PAD, channels)

    def dma(*shape):
        return pltpu.SemaphoreType.DMA(shape)

    mixed, grad_input, total = pl.pallas_call(
        functools.partial(kernel, scale, lon, pairs, q),
        out_shape=(
            jax.ShapeDtypeStruct(features.shape, bf16),
            jax.ShapeDtypeStruct(features.shape, bf16),
            jax.ShapeDtypeStruct((K * channels, channels), bf16),
        ),
        in_specs=[anywhere, anywhere, vmem, smem, smem, anywhere],
        out_specs=[anywhere, anywhere, vmem],
        scratch_shapes=[
            pltpu.VMEM(wide, bf16),
            pltpu.VMEM(wide, bf16),
            pltpu.VMEM((rows + 2 * RAD, SUB, LANES), f32),
            pltpu.VMEM((K * channels, channels), bf16),
            pltpu.VMEM((K * channels, channels), bf16),
            pltpu.VMEM((WIDTH, rows, SUB, 256), f32),
            pltpu.VMEM((WIDTH, rows + 2 * RAD, SUB, 256), f32),
            pltpu.VMEM((rows, K * J, 256), bf16),
            pltpu.VMEM((rows, K * J, 256), bf16),
            pltpu.VMEM((rows, lon_count, K * channels), bf16),
            pltpu.VMEM((channels, rows * lon_count), bf16),
            pltpu.VMEM(features.shape, bf16),
            pltpu.VMEM(features.shape, bf16),
            pltpu.VMEM((chunks, groups, SUB, LANES), f32),
            pltpu.VMEM((chunks, groups, SUB, LANES), bf16),
            dma(5), dma(9), dma(9), dma(9), dma(9), dma(2), dma(2),
            pltpu.VMEM((chunks, lon * piece, SUB, LANES), f32),
            pltpu.VMEM((chunks, lon - 1, piece, SUB, LANES), bf16),
            pltpu.VMEM((chunks, lon - 1, piece, SUB, LANES), bf16),
            pltpu.VMEM((chunks, piece, SUB, LANES), f32),
            pltpu.VMEM((chunks, pairs - 1, q, SUB, LANES), bf16),
            pltpu.VMEM((chunks, pairs - 1, q, SUB, LANES), bf16),
            dma(chunks, lon), dma(chunks, lon),
            dma(chunks, lon - 1), dma(chunks, lon - 1),
            dma(chunks, pairs - 1), dma(chunks, pairs - 1),
            dma(chunks, pairs - 1), dma(chunks, pairs - 1),
            dma(chunks, pairs, lon - 1), dma(chunks, pairs, lon - 1),
            dma(chunks, lon), dma(chunks, lon),
        ],
        compiler_params=pltpu.CompilerParams(
            collective_id=0, has_side_effects=True, vmem_limit_bytes=60 * 2**20
        ),
    )(features, cotangent, basis, span_lo, span_hi, weight.reshape(K * channels, channels))
    return (mixed, grad_input, total.reshape(weight.shape).astype(f32))


def solution(mesh):
    return jax.shard_map(
        per_device,
        mesh=mesh,
        in_specs=(
            P("lat", "lon", None),
            P("lat", None, None),
            P("lat"),
            P("lat"),
            P(),
            P("lat", "lon", None),
        ),
        out_specs=(P("lat", "lon", None), P("lat", "lon", None), P()),
        check_vma=False,
    )
```

time: 59.3 us -> 54.2 us (0.914)
  Pallas kernels: 50.8 us -> 46.3 us
  other arithmetic: 4.38 us -> 2.98 us
  local copies, waits for them, and re-layouts: 3.17 us -> 3.92 us
    pallas_call x1, Pallas kernels: 50.8 us -> 46.3 us  [per_device(): pl.pallas_call(functools.partial(kernel, scale, lon, pairs, q), out_shape...]
    convert_element_type x0 -> x1, other arithmetic: none -> 2.98 us  [per_device(): return (mixed, grad_input, total.reshape(weight.shape).astype(f32))]
    reshape x1 -> x0, other arithmetic: 2.89 us -> none  [per_device(): grad_weight = jnp.swapaxes(total, 1, 2).reshape(weight.shape)]
    unnamed x4 -> x7, local copies, waits for them, and re-layouts: 3.16 us -> 3.92 us
    and x1 -> x0, other arithmetic: 0.75 us -> none  [kept_basis(): (offsets[None, :] >= span_lo[:, None]) & (offsets[None, :] <= span_hi[:,...]
    select_n x1 -> x0, other arithmetic: 0.73 us -> none  [kept_basis(): return jnp.where(keep[:, None, :], basis, jnp.zeros_like(basis))]
where the time goes in v4:
time: 54.2 us; the launch traced here: 53.9 us
  Pallas kernels  46.3 us (85%)
  local copies, waits for them, and re-layouts  3.92 us (7%)
  other arithmetic  2.98 us (5%)
  between operations  0.65 us (1%)
    pallas_call x1, Pallas kernels, per_device(): pl.pallas_call(functools.partial(kernel, scale, lon, pairs, q), out_shape...  46.3 us
    unnamed x7, local copies, waits for them, and re-layouts  3.92 us
    convert_element_type x1, other arithmetic, per_device(): return (mixed, grad_input, total.reshape(weight.shape).astype(f32))  2.98 us

profile of v4, /device:TPU:0, one launch (start us, length us, event | category | flops | bytes accessed | tf_op | source)
XLA Modules:
  0.0 53.9 jit_solution(5966972935375053710)
XLA Ops:
  0.6 1.3 %copy.9.basis_ref = f32[4,9,25]{2,1,0:T(8,128)} copy(f32[4,9,25]{2,0,1:T(4,128)} %param.7) | data formatting | bytes 7200 | tf_op args[1]
  2.0 46.3 %shard_map.85 = (bf16[4,512,256]{2,1,0:T(8,128)(2,1)}, bf16[4,512,256]{2,1,0:T(8,128)(2,1)}, bf16[2304,256]{1,0:T(8,128)(2,1)}) custom-call(bf16[4,512,256]{2,1,0:T(8,128)(2,1)} %f_ref.1, bf16[4,512,256]{2,1,0:T(8,128)(2,1)} %c_ref.1, f32[4,9,25]{2,1,0:T(8,128)} %copy.9.basis_ref, s32[4]{0:T(128)} %lo_ref.1, s32[4]{0:T(128)} %hi_ref.1, bf16[2304,256]{1,0:T(8,128)(2,1)} %bitcast.4), custom_call_target="tpu_custom_call" | custom-call | tf_op jit(solution)/shard_map/pallas_call | solution.py:459
  48.3 0.0 copy-start.1
  48.3 3.0 %convert.1 = f32[9,256,256]{2,1,0:T(8,128)} convert(bf16[9,256,256]{2,1,0:T(8,128)(2,1)} %bitcast.3) | non-fusion elementwise | flops 589824 | bytes 3538944 | tf_op jit(solution)/shard_map/convert_element_type | solution.py:502
  51.3 0.0 copy-done.1
  51.3 0.0 copy-start
  51.3 1.0 %copy.12 = bf16[4,512,256]{2,1,0:T(8,128)(2,1)} copy(bf16[4,512,256]{2,1,0:T(8,128)(2,1)S(1)} %copy-done.1) | data formatting | bytes 2097152
  52.3 0.6 %copy-done = bf16[4,512,256]{2,1,0:T(8,128)(2,1)S(1)} copy-done((bf16[4,512,256]{2,1,0:T(8,128)(2,1)S(1)}, bf16[4,512,256]{2,1,0:T(8,128)(2,1)}, u32[]{:S(2)}) %copy-start) | copy-done | bytes 1048600
  52.9 1.0 %copy.13 = bf16[4,512,256]{2,1,0:T(8,128)(2,1)} copy(bf16[4,512,256]{2,1,0:T(8,128)(2,1)S(1)} %copy-done) | data formatting | bytes 2097152
Async XLA Ops:
  48.3 3.0 %copy-start.1 = (bf16[4,512,256]{2,1,0:T(8,128)(2,1)S(1)}, bf16[4,512,256]{2,1,0:T(8,128)(2,1)}, u32[]{:S(2)}) copy-start(bf16[4,512,256]{2,1,0:T(8,128)(2,1)} %get-tuple-element.12) | copy-start | bytes 3145732
  51.3 1.6 %copy-start = (bf16[4,512,256]{2,1,0:T(8,128)(2,1)S(1)}, bf16[4,512,256]{2,1,0:T(8,128)(2,1)}, u32[]{:S(2)}) copy-start(bf16[4,512,256]{2,1,0:T(8,128)(2,1)} %get-tuple-element.13) | copy-start | bytes 3145732

commit v5 on v4

--- a/solution.py
+++ b/solution.py
@@ -193,7 +193,7 @@
 def kernel(
     scale, lon, pairs, q, f_ref, c_ref, basis_ref, lo_ref, hi_ref, w_hbm, mixed_hbm, gi_hbm, gw_ref,
     fx, cx, bx, w_ref, wt_ref, v_ref, u_ref, fa_ref, ca_ref, y_ref, ct_ref, mixed_ref, gi_ref,
-    groups_ref, sums_ref, local_sem, f_send, f_recv, c_send, c_recv, b_send, b_recv, *reduce_scratch,
+    acc_ref, groups_ref, sums_ref, local_sem, f_send, f_recv, c_send, c_recv, b_send, b_recv, *reduce_scratch,
 ):
     rows, lon_count, channels = f_ref.shape
     lat, n = lax.axis_index("lat"), lax.axis_index("lon")
@@ -228,7 +228,7 @@
     bx[here] = jnp.zeros((rows,) + bx.shape[1:], jnp.float32)
     for i in range(rows):
         keep = (offset >= lo_ref[i]) & (offset <= hi_ref[i])
-        bx[RAD + i, 0:K, 0:TAPS] = jnp.where(keep, basis_ref[i], 0.0)
+        bx[RAD + i, 0:K, 0:TAPS] = jnp.where(keep, basis_ref[:, i, :], 0.0)
     for dy, edge in ((1, 0), (-1, RAD + rows)):
         @pl.when(jnp.logical_not(has[-dy]))
         def _():
@@ -240,7 +240,6 @@
         3 * has[1].astype(jnp.int32) + 3 * has[-1].astype(jnp.int32) + lon - 1 + pairs - 1,
     )
 
-    f_near, f_far, f_sent = halo_starts(f_ref, fx, f_send, f_recv)
     b_copies = {}
     for slot, dy, src, dst in ((0, 1, rows, 0), (1, -1, RAD, RAD + rows)):
         b_copies[dy] = pltpu.make_async_remote_copy(
@@ -252,6 +251,8 @@
         @pl.when(has[dy])
         def _():
             b_copies[dy].start()
+
+    f_near, f_far, f_sent = halo_starts(f_ref, fx, f_send, f_recv)
 
     taps = lax.broadcasted_iota(jnp.int32, (LANES, 256), 0)
 
@@ -339,9 +340,23 @@
     looped(first_near, first_near + halfway, lambda i: stencil(fx, fa_ref, i))
     locals_[1].wait()
     for i in range(rows):
-        ct_ref[:, i * lon_count : (i + 1) * lon_count] = cx[RAD + i, PAD : PAD + lon_count].T
+        ct_ref[i] = cx[RAD + i, PAD : PAD + lon_count].T
+
+    def product(k, first):
+        column = slice(k * channels, (k + 1) * channels)
+        total = jnp.zeros((channels, channels), jnp.float32)
+        for r in range(halfway):
+            total += jnp.dot(
+                ct_ref[first + r], y_ref[first + r, :, column], preferred_element_type=jnp.float32
+            )
+        return total
+
+    for k in range(K):
+        acc_ref[k] = product(k, first_near)
     locals_[2].wait()
-    looped(first_near, first_near + halfway, lambda i: mix(i, w_ref, mixed_ref))
+    for k in range(K):
+        block = slice(k * channels, (k + 1) * channels)
+        wt_ref[block] = w_ref[block].T
     f_far()
     c_near, c_far, c_sent = halo_starts(c_ref, cx, c_send, c_recv)
     looped(first_far, first_far + halfway, lambda i: stencil(fx, fa_ref, i))
@@ -352,17 +367,10 @@
     halves = channels // LANES
     used = each * halves * per
 
-    def product(m):
+    def chunk(m):
         for j in range(each):
             k = m * each + j
-            total = jnp.zeros((channels, channels), jnp.float32)
-            for i in range(rows):
-                total += jnp.dot(
-                    ct_ref[:, i * lon_count : (i + 1) * lon_count],
-                    y_ref[i, :, k * channels : (k + 1) * channels],
-                    preferred_element_type=jnp.float32,
-                )
-            turned = total.T * scale
+            turned = (acc_ref[k] + product(k, first_far)).T * scale
             for h in range(halves):
                 at = (j * halves + h) * per
                 block = turned[:, h * LANES : (h + 1) * LANES]
@@ -400,20 +408,17 @@
         stencil(cx, ca_ref, i)
         mix(i, wt_ref, gi_ref)
 
-    product(0)
+    chunk(0)
     go(0)
-    product(1)
+    chunk(1)
     go(1, 0)
-    product(2)
+    chunk(2)
     go(2, 1)
-    looped(first_far, first_far + 1, lambda i: mix(i, w_ref, mixed_ref))
+    looped(first_near, first_near + halfway, lambda i: mix(i, w_ref, mixed_ref))
     go(2, 0)
-    looped(first_far + 1, first_far + halfway, lambda i: mix(i, w_ref, mixed_ref))
+    looped(first_far, first_far + halfway, lambda i: mix(i, w_ref, mixed_ref))
     out_copies[0].start()
     go(1, 0)
-    for k in range(K):
-        block = slice(k * channels, (k + 1) * channels)
-        wt_ref[block] = w_ref[block].T
     build_adjoint()
     go(2, 1, 0)
     c_near()
@@ -439,6 +444,28 @@
         copy.wait()
 
 
+def finish_kernel(
+    mixed_in, gi_in, sums_in, mixed_out, gi_out, gw_out, narrow, wide, moved, loaded, stored
+):
+    loads = [pltpu.make_async_copy(sums_in.at[k], narrow.at[k], loaded.at[k]) for k in range(K)]
+    for copy in loads:
+        copy.start()
+    moves = [
+        pltpu.make_async_copy(mixed_in, mixed_out, moved.at[0]),
+        pltpu.make_async_copy(gi_in, gi_out, moved.at[1]),
+    ]
+    for copy in moves:
+        copy.start()
+    stores = []
+    for k in range(K):
+        loads[k].wait()
+        wide[k] = narrow[k].astype(jnp.float32)
+        stores.append(pltpu.make_async_copy(wide.at[k], gw_out.at[k], stored.at[k]))
+        stores[k].start()
+    for copy in moves + stores:
+        copy.wait()
+
+
 def per_device(features, basis, span_lo, span_hi, weight, cotangent):
     rows, lon_count, channels = features.shape
     scale = 1.0 / math.sqrt(rows * lax.axis_size("lat") * lon_count * lax.axis_size("lon"))
@@ -476,9 +503,10 @@
             pltpu.VMEM((rows, K * J, 256), bf16),
             pltpu.VMEM((rows, K * J, 256), bf16),
             pltpu.VMEM((rows, lon_count, K * channels), bf16),
-            pltpu.VMEM((channels, rows * lon_count), bf16),
+            pltpu.VMEM((rows, channels, lon_count), bf16),
             pltpu.VMEM(features.shape, bf16),
             pltpu.VMEM(features.shape, bf16),
+            pltpu.VMEM((K, channels, channels), f32),
             pltpu.VMEM((chunks, groups, SUB, LANES), f32),
             pltpu.VMEM((chunks, groups, SUB, LANES), bf16),
             dma(5), dma(9), dma(9), dma(9), dma(9), dma(2), dma(2),
@@ -498,8 +526,23 @@
         compiler_params=pltpu.CompilerParams(
             collective_id=0, has_side_effects=True, vmem_limit_bytes=60 * 2**20
         ),
-    )(features, cotangent, basis, span_lo, span_hi, weight.reshape(K * channels, channels))
-    return (mixed, grad_input, total.reshape(weight.shape).astype(f32))
+    )(features, cotangent, jnp.swapaxes(basis, 0, 1), span_lo, span_hi, weight.reshape(K * channels, channels))
+    return pl.pallas_call(
+        finish_kernel,
+        out_shape=(
+            jax.ShapeDtypeStruct(features.shape, bf16),
+            jax.ShapeDtypeStruct(features.shape, bf16),
+            jax.ShapeDtypeStruct(weight.shape, f32),
+        ),
+        in_specs=[anywhere] * 3,
+        out_specs=[anywhere] * 3,
+        scratch_shapes=[
+            pltpu.VMEM(weight.shape, bf16),
+            pltpu.VMEM(weight.shape, f32),
+            dma(2), dma(K), dma(K),
+        ],
+        compiler_params=pltpu.CompilerParams(vmem_limit_bytes=60 * 2**20),
+    )(mixed, grad_input, total.reshape(weight.shape))
 
 
 def solution(mesh):

time: 54.2 us -> 111 us (2.05)
  Pallas kernels: 46.3 us -> 110 us
  local copies, waits for them, and re-layouts: 3.92 us -> 0 us
  other arithmetic: 2.98 us -> 0 us
    pallas_call x0 -> x1, Pallas kernels: none -> 64.8 us  [per_device(): pl.pallas_call(finish_kernel, out_shape=(jax.ShapeDtypeStruct(features.sh...]
    unnamed x7 -> x0, local copies, waits for them, and re-layouts: 3.92 us -> none
    convert_element_type x1 -> x0, other arithmetic: 2.98 us -> none  [per_device(): return (mixed, grad_input, total.reshape(weight.shape).astype(f32))]
where the time goes in v5:
time: 111 us
  Pallas kernels  110 us (99%)
    pallas_call x1, Pallas kernels, per_device(): pl.pallas_call(finish_kernel, out_shape=(jax.ShapeDtypeStruct(features.sh...  64.8 us
    pallas_call x1, Pallas kernels, per_device(): pl.pallas_call(functools.partial(kernel, scale, lon, pairs, q), out_shape...  45.6 us

profile of v5, /device:TPU:0, one launch (start us, length us, event | category | flops | bytes accessed | tf_op | source)
XLA Modules:
  0.0 111.1 jit_solution(10951025286100670113)
XLA Ops:
  0.6 45.6 %shard_map.85 = (bf16[4,512,256]{2,1,0:T(8,128)(2,1)}, bf16[4,512,256]{2,1,0:T(8,128)(2,1)}, bf16[2304,256]{1,0:T(8,128)(2,1)}) custom-call(bf16[4,512,256]{2,1,0:T(8,128)(2,1)} %f_ref.1, bf16[4,512,256]{2,1,0:T(8,128)(2,1)} %c_ref.1, f32[9,4,25]{2,1,0:T(4,128)} %bitcast.5, s32[4]{0:T(128)} %lo_ref.1, s32[4]{0:T(128)} %hi_ref.1, bf16[2304,256]{1,0:T(8,128)(2,1)} %bitcast.4), custom_call_target="tpu_custom_call" | custom-call | tf_op jit(solution)/shard_map/pallas_call | solution.py:486
  46.2 64.8 %shard_map.86 = (bf16[4,512,256]{2,1,0:T(8,128)(2,1)}, bf16[4,512,256]{2,1,0:T(8,128)(2,1)}, f32[9,256,256]{2,1,0:T(8,128)}) custom-call(bf16[4,512,256]{2,1,0:T(8,128)(2,1)} %get-tuple-element.6.mixed_in, bf16[4,512,256]{2,1,0:T(8,128)(2,1)} %get-tuple-element.7.gi_in, bf16[9,256,256]{2,1,0:T(8,128)(2,1)} %bitcast.3), custom_call_target="tpu_custom_call" | custom-call | tf_op jit(solution)/shard_map/pallas_call | solution.py:530

commit v6 on v5

--- a/solution.py
+++ b/solution.py
@@ -445,24 +445,28 @@
 
 
 def finish_kernel(
-    mixed_in, gi_in, sums_in, mixed_out, gi_out, gw_out, narrow, wide, moved, loaded, stored
+    mixed_in, gi_in, sums_in, mixed_out, gi_out, gw_out, mixed, gi, narrow, wide,
+    moved_in, moved_out, loaded, stored,
 ):
-    loads = [pltpu.make_async_copy(sums_in.at[k], narrow.at[k], loaded.at[k]) for k in range(K)]
-    for copy in loads:
+    rows = mixed.shape[0]
+    loads, stores = [], []
+    for a, (src, held, dst) in enumerate(((mixed_in, mixed, mixed_out), (gi_in, gi, gi_out))):
+        for i in range(rows):
+            loads.append(pltpu.make_async_copy(src.at[i], held.at[i], moved_in.at[a, i]))
+            stores.append(pltpu.make_async_copy(held.at[i], dst.at[i], moved_out.at[a, i]))
+    sums = [pltpu.make_async_copy(sums_in.at[k], narrow.at[k], loaded.at[k]) for k in range(K)]
+    for copy in sums + loads:
         copy.start()
-    moves = [
-        pltpu.make_async_copy(mixed_in, mixed_out, moved.at[0]),
-        pltpu.make_async_copy(gi_in, gi_out, moved.at[1]),
-    ]
-    for copy in moves:
+    for k in range(K):
+        sums[k].wait()
+        wide[k] = narrow[k].astype(jnp.float32)
+        copy = pltpu.make_async_copy(wide.at[k], gw_out.at[k], stored.at[k])
         copy.start()
-    stores = []
-    for k in range(K):
-        loads[k].wait()
-        wide[k] = narrow[k].astype(jnp.float32)
-        stores.append(pltpu.make_async_copy(wide.at[k], gw_out.at[k], stored.at[k]))
-        stores[k].start()
-    for copy in moves + stores:
+        stores.append(copy)
+    for i, copy in enumerate(loads):
+        copy.wait()
+        stores[i].start()
+    for copy in stores:
         copy.wait()
 
 
@@ -537,9 +541,11 @@
         in_specs=[anywhere] * 3,
         out_specs=[anywhere] * 3,
         scratch_shapes=[
+            pltpu.VMEM(features.shape, bf16),
+            pltpu.VMEM(features.shape, bf16),
             pltpu.VMEM(weight.shape, bf16),
             pltpu.VMEM(weight.shape, f32),
-            dma(2), dma(K), dma(K),
+            dma(2, rows), dma(2, rows), dma(K), dma(K),
         ],
         compiler_params=pltpu.CompilerParams(vmem_limit_bytes=60 * 2**20),
     )(mixed, grad_input, total.reshape(weight.shape))

time: 111 us -> 50 us (0.45)
  Pallas kernels: 110 us -> 49.2 us
    pallas_call x1, Pallas kernels: 64.8 us -> 3.57 us  [per_device(): pl.pallas_call(finish_kernel, out_shape=(jax.ShapeDtypeStruct(features.sh...]
where the time goes in v6:
time: 50 us; the launch traced here: 49.8 us
  Pallas kernels  49.2 us (98%)
  between operations  0.64 us (1%)
    pallas_call x1, Pallas kernels, per_device(): pl.pallas_call(functools.partial(kernel, scale, lon, pairs, q), out_shape...  45.6 us
    pallas_call x1, Pallas kernels, per_device(): pl.pallas_call(finish_kernel, out_shape=(jax.ShapeDtypeStruct(features.sh...  3.57 us

profile of v6, /device:TPU:0, one launch (start us, length us, event | category | flops | bytes accessed | tf_op | source)
XLA Modules:
  0.0 49.8 jit_solution(914429273079854624)
XLA Ops:
  0.6 45.6 %shard_map.85 = (bf16[4,512,256]{2,1,0:T(8,128)(2,1)}, bf16[4,512,256]{2,1,0:T(8,128)(2,1)}, bf16[2304,256]{1,0:T(8,128)(2,1)}) custom-call(bf16[4,512,256]{2,1,0:T(8,128)(2,1)} %f_ref.1, bf16[4,512,256]{2,1,0:T(8,128)(2,1)} %c_ref.1, f32[9,4,25]{2,1,0:T(4,128)} %bitcast.5, s32[4]{0:T(128)} %lo_ref.1, s32[4]{0:T(128)} %hi_ref.1, bf16[2304,256]{1,0:T(8,128)(2,1)} %bitcast.4), custom_call_target="tpu_custom_call" | custom-call | tf_op jit(solution)/shard_map/pallas_call | solution.py:490
  46.2 3.6 %shard_map.86 = (bf16[4,512,256]{2,1,0:T(8,128)(2,1)}, bf16[4,512,256]{2,1,0:T(8,128)(2,1)}, f32[9,256,256]{2,1,0:T(8,128)}) custom-call(bf16[4,512,256]{2,1,0:T(8,128)(2,1)} %get-tuple-element.6.mixed_in, bf16[4,512,256]{2,1,0:T(8,128)(2,1)} %get-tuple-element.7.gi_in, bf16[9,256,256]{2,1,0:T(8,128)(2,1)} %bitcast.3), custom_call_target="tpu_custom_call" | custom-call | tf_op jit(solution)/shard_map/pallas_call | solution.py:534

commit v7 on v6

--- a/solution.py
+++ b/solution.py
@@ -89,13 +89,6 @@
 
     d_copies, e_copies, f_copies = [], [], []
 
-    def to_lon(t):
-        src = out_ref.at[pl.ds(own + lax.rem(z + pairs - t, pairs) * q, q)]
-        for s in range(lon - 1):
-            e_copies.append(
-                remote(src, src, e_send.at[t, s], e_recv.at[t, s], (lat, lon_peer(s + 1)))
-            )
-
     def to_partner(s, p):
         src = out_ref.at[pl.ds(mine + p * piece, piece)]
         f_copies.append(remote(src, src, f_send.at[s], f_recv.at[s], partner))
@@ -105,16 +98,16 @@
         d_copies.append(
             remote(src, src, d_send.at[s], d_recv.at[s], (pair_peer(s + 1) * 2 + core, n))
         )
-    to_lon(0)
     yield
-    for t in range(1, pairs):
-        d_copies[t - 1].wait_recv()
-        to_lon(t)
+    for copy in d_copies:
+        copy.wait_recv()
+    src = out_ref.at[pl.ds(own, piece)]
+    for s in range(lon - 1):
+        e_copies.append(remote(src, src, e_send.at[s], e_recv.at[s], (lat, lon_peer(s + 1))))
     to_partner(0, n)
     yield
     for s in range(lon - 1):
-        for t in range(pairs):
-            e_copies[t * (lon - 1) + s].wait_recv()
+        e_copies[s].wait_recv()
         to_partner(s + 1, lax.rem(n + lon - s - 1, lon))
     yield
     for copy in f_copies:
@@ -524,7 +517,7 @@
             dma(chunks, lon - 1), dma(chunks, lon - 1),
             dma(chunks, pairs - 1), dma(chunks, pairs - 1),
             dma(chunks, pairs - 1), dma(chunks, pairs - 1),
-            dma(chunks, pairs, lon - 1), dma(chunks, pairs, lon - 1),
+            dma(chunks, lon - 1), dma(chunks, lon - 1),
             dma(chunks, lon), dma(chunks, lon),
         ],
         compiler_params=pltpu.CompilerParams(

time: 50 us -> 50.2 us (level)
  no operation moved by 1% of the time
where the time goes in v7:
time: 50.2 us; the launch traced here: 50 us
  Pallas kernels  49.4 us (98%)
  between operations  0.64 us (1%)
    pallas_call x1, Pallas kernels, per_device(): pl.pallas_call(functools.partial(kernel, scale, lon, pairs, q), out_shape...  45.8 us
    pallas_call x1, Pallas kernels, per_device(): pl.pallas_call(finish_kernel, out_shape=(jax.ShapeDtypeStruct(features.sh...  3.57 us

profile of v7, /device:TPU:0, one launch (start us, length us, event | category | flops | bytes accessed | tf_op | source)
XLA Modules:
  0.0 50.0 jit_solution(1244600729916735588)
XLA Ops:
  0.6 45.8 %shard_map.85 = (bf16[4,512,256]{2,1,0:T(8,128)(2,1)}, bf16[4,512,256]{2,1,0:T(8,128)(2,1)}, bf16[2304,256]{1,0:T(8,128)(2,1)}) custom-call(bf16[4,512,256]{2,1,0:T(8,128)(2,1)} %f_ref.1, bf16[4,512,256]{2,1,0:T(8,128)(2,1)} %c_ref.1, f32[9,4,25]{2,1,0:T(4,128)} %bitcast.5, s32[4]{0:T(128)} %lo_ref.1, s32[4]{0:T(128)} %hi_ref.1, bf16[2304,256]{1,0:T(8,128)(2,1)} %bitcast.4), custom_call_target="tpu_custom_call" | custom-call | tf_op jit(solution)/shard_map/pallas_call | solution.py:483
  46.5 3.6 %shard_map.86 = (bf16[4,512,256]{2,1,0:T(8,128)(2,1)}, bf16[4,512,256]{2,1,0:T(8,128)(2,1)}, f32[9,256,256]{2,1,0:T(8,128)}) custom-call(bf16[4,512,256]{2,1,0:T(8,128)(2,1)} %get-tuple-element.6.mixed_in, bf16[4,512,256]{2,1,0:T(8,128)(2,1)} %get-tuple-element.7.gi_in, bf16[9,256,256]{2,1,0:T(8,128)(2,1)} %bitcast.3), custom_call_target="tpu_custom_call" | custom-call | tf_op jit(solution)/shard_map/pallas_call | solution.py:527
